TPU v7x, 128 devices: a whole 4x4x4 slice. The times are simulated.
128 devices in a mesh: dp: 16 (over z, x_lo, core), tensor: 8 (over x_hi, y).
Axes of the slice: x: 4 (x_hi: 2, x_lo: 2; x = x_hi * 2 + x_lo), y: 4, z: 4, core: 2. Of those that a mesh axis runs over, the one named last changes fastest.
Arguments:
- tokens: bfloat16 [24576, 1536], P(('dp', 'tensor')), may hold values from -24 to 24
- gain_attn: float32 [1536], replicated, may hold values from 0.5 to 1.5
- gain_mlp: float32 [1536], replicated, may hold values from 0.5 to 1.5
- w_query: bfloat16 [1536, 1536], P('dp', 'tensor'), may hold values from -0.15625 to 0.15625
- w_key: bfloat16 [1536, 768], P('dp', 'tensor'), may hold values from -0.15625 to 0.15625
- w_value: bfloat16 [1536, 768], P('dp', 'tensor'), may hold values from -0.15625 to 0.15625
- w_out: bfloat16 [1536, 1536], P(('tensor', 'dp')), may hold values from -1.25 to 1.25
- w_gate: bfloat16 [1536, 4096], P('dp', 'tensor'), may hold values from -0.15625 to 0.15625
- w_up: bfloat16 [1536, 4096], P('dp', 'tensor'), may hold values from -0.15625 to 0.15625
- w_down: bfloat16 [4096, 1536], P(('tensor', 'dp')), may hold values from -0.09375 to 0.09375
- segments: int32 [24576], P('dp'), may hold values from 0 to 24575, as said below
- positions: int32 [24576], P('dp'), may hold values from 0 to 1999, as said below
- cotangent: bfloat16 [24576, 1536], P(('dp', 'tensor')), may hold values from -6 to 6
Outputs:
- result: bfloat16 [24576, 1536], P(('dp', 'tensor'))
- token_grad: bfloat16 [24576, 1536], P(('dp', 'tensor'))
- grad_gain_attn: float32 [1536], replicated
- grad_gain_mlp: float32 [1536], replicated
- grad_query: float32 [1536, 1536], P('dp', 'tensor')
- grad_key: float32 [1536, 768], P('dp', 'tensor')
- grad_value: float32 [1536, 768], P('dp', 'tensor')
- grad_out: float32 [1536, 1536], P(('tensor', 'dp'))
- grad_gate: float32 [1536, 4096], P('dp', 'tensor')
- grad_up: float32 [1536, 4096], P('dp', 'tensor')
- grad_down: float32 [4096, 1536], P(('tensor', 'dp'))
Inputs may be any that keep to these rules, and one draw needn't show every extreme that they name: `segments`: segment labels never fall along the tokens; each run of equal labels is one document of 200 to 2000 tokens (the last one may be cut short), documents run on across sequences, and different documents have different labels. positions counts from 0 at the first token of each document and rises by one along it.
All inputs are finite; a program needn't handle non-finite values.
Results may differ from a plain program's by a relative error of at most 0.025.
Values may be sent and summed in bfloat16 or wider, within the bound.
A program may use at most 128 MiB of HBM per device.

v0:
```python
import functools
import math

import jax
import jax.numpy as jnp
from jax import lax
from jax.experimental import pallas as pl
from jax.experimental.pallas import tpu as pltpu
from jax.sharding import PartitionSpec as P

HD = 96
SEQ = 512
D = 1536
OWN = 192
HALF = 768
WIN = 256

EPSILON = 1e-05
ROPE_BASE = 100000.0
MASKED = -1e30
MESH = pl.DeviceIdType.MESH
ANY = pl.BlockSpec(memory_space=pl.ANY)
VMEM = pl.BlockSpec(memory_space=pltpu.VMEM)
BF16 = jnp.bfloat16
F32 = jnp.float32


def place():
    dp = lax.axis_index("dp")
    tensor = lax.axis_index("tensor")
    return (tensor // 4) * 2 + (dp // 2) % 2, tensor % 4, dp // 4, dp % 2


def device(x, y, z, c):
    return (z * 4 + (x % 2) * 2 + c, (x // 2) * 4 + y)


def turn(pos, by):
    return (pos + by + 4) % 4


class Spot:
    def __init__(self):
        x, y, z, c = place()
        self.x, self.y, self.z, self.c = x, y, z, c
        self.high, self.low = x // 2, x % 2
        self.quad = self.low * 2 + c
        self.sibling = device(x, y, z, 1 - c)
        self.partner = device(turn(x, 2), y, z, 1 - c)

    def along(self, axis, by):
        x, y, z, c = self.x, self.y, self.z, self.c
        if axis == "x":
            return device(turn(x, by), y, z, c)
        if axis == "y":
            return device(x, turn(y, by), z, c)
        return device(x, y, turn(z, by), c)

    def me(self, axis):
        return {"x": self.x, "y": self.y, "z": self.z}[axis]

    def in_quad(self, by):
        other = turn(self.quad, by)
        return other, device(self.high * 2 + other // 2, self.y, self.z, other % 2)


def greet(devices):
    barrier = pltpu.get_barrier_semaphore()
    for who in devices:
        pl.semaphore_signal(barrier, inc=1, device_id=who, device_id_type=MESH)
    pl.semaphore_wait(barrier, len(devices))


class Wires:
    def __init__(self, send_sem, recv_sem):
        self.send_sem, self.recv_sem = send_sem, recv_sem
        self.count = 0
        self.sent = []
        self.moved = []

    def send(self, src, dst, who):
        copy = pltpu.make_async_remote_copy(
            src_ref=src,
            dst_ref=dst,
            send_sem=self.send_sem.at[self.count],
            recv_sem=self.recv_sem.at[self.count],
            device_id=who,
            device_id_type=MESH,
        )
        self.count += 1
        copy.start()
        self.sent.append(copy)
        return copy

    def move(self, src, dst):
        copy = pltpu.make_async_copy(src, dst, self.send_sem.at[self.count])
        self.count += 1
        copy.start()
        return copy

    def done(self, copies):
        for copy in copies:
            if any(other is copy for other in self.sent):
                self.sent = [other for other in self.sent if other is not copy]
                copy.wait_send()

    def close(self):
        self.done(list(self.sent))


def add_into(dst, *srcs, chunk=16):
    rows = dst.shape[-2]
    chunk = min(chunk, rows)

    def step(i, carry):
        span = pl.ds(pl.multiple_of(i * chunk, chunk), chunk)
        total = srcs[0][..., span, :].astype(F32)
        for src in srcs[1:]:
            total = total + src[..., span, :].astype(F32)
        dst[..., span, :] = total.astype(dst.dtype)
        return carry

    lax.fori_loop(0, rows // chunk, step, 0)


class RingGather:
    def __init__(self, wires, spot, axis, at):
        self.wires, self.at = wires, at
        self.me = spot.me(axis)
        self.next, self.prev = spot.along(axis, 1), spot.along(axis, -1)

    def start(self, own=None):
        own = own or (lambda half: self.at(self.me, half))
        send, at, me = self.wires.send, self.at, self.me
        self.right0 = send(own(0), at(me, 0), self.next)
        self.left1 = send(own(1), at(me, 1), self.prev)
        self.right1 = send(own(1), at(me, 1), self.next)
        self.left0 = send(own(0), at(me, 0), self.prev)

    def forward(self):
        send, at, me = self.wires.send, self.at, self.me
        self.right0.wait_recv()
        before = at(turn(me, -1), 0)
        self.pass0 = send(before, before, self.next)
        self.left1.wait_recv()
        after = at(turn(me, 1), 1)
        self.pass1 = send(after, after, self.prev)

    def near(self):
        self.right1.wait_recv()
        self.left0.wait_recv()

    def far(self):
        self.pass0.wait_recv()
        self.pass1.wait_recv()

    def close(self):
        near = [self.right0, self.left1, self.right1, self.left0]
        self.wires.done(near + [self.pass0, self.pass1])


class PairGather:
    def __init__(self, wires, spot, axis, out, own, start, size):
        self.wires, self.spot, self.out, self.own = wires, spot, out, own
        self.rows = pl.ds(start, size)
        cut = size // 2

        def half_rows(half):
            return pl.ds(start + half * cut, cut)

        self.half_rows = half_rows
        self.ring = RingGather(
            wires, spot, axis, lambda pos, half: out.at[spot.c, pos, half_rows(half)]
        )
        self.me = spot.me(axis)

    def share(self, pos):
        block = self.out.at[self.spot.c, pos, self.rows]
        return self.wires.send(block, block, self.spot.sibling)

    def start(self):
        self.ring.start(lambda half: self.own.at[self.half_rows(half)])
        mine = self.own.at[self.rows]
        place_of = self.out.at[self.spot.c, self.me, self.rows]
        self.shared = [self.wires.send(mine, place_of, self.spot.sibling)]
        self.kept = self.wires.move(mine, place_of)

    def forward(self):
        self.ring.forward()
        self.ring.near()
        self.shared.append(self.share(turn(self.me, -1)))
        self.shared.append(self.share(turn(self.me, 1)))

    def far(self):
        self.ring.far()
        self.shared.append(self.share(turn(self.me, 2)))

    def finish(self):
        for copy in self.shared:
            copy.wait_recv()
        self.kept.wait()

    def close(self):
        self.ring.close()
        self.wires.done(self.shared)


class PairScatter:
    def __init__(self, wires, spot, axis, part, got, passed, near, start, size):
        self.wires, self.spot = wires, spot
        self.me = spot.me(axis)
        self.next, self.prev = spot.along(axis, 1), spot.along(axis, -1)
        self.part, self.got, self.passed, self.near = part, got, passed, near
        self.start_row, self.size, self.cut = start, size, size // 2
        self.shared = {}

    def rows(self, half=None):
        if half is None:
            return pl.ds(self.start_row, self.size)
        return pl.ds(self.start_row + half * self.cut, self.cut)

    def share(self, by):
        pos = turn(self.me, by)
        self.shared[by] = self.wires.send(
            self.part.at[1 - self.spot.c, pos, self.rows()],
            self.got.at[pos, self.rows()],
            self.spot.sibling,
        )

    def first(self):
        self.shared[2].wait_recv()
        pos = turn(self.me, 2)
        mine = self.got.at[pos, self.rows()]
        add_into(mine, self.part.at[self.spot.c, pos, self.rows()], mine)
        self.pass0 = self.wires.send(
            self.got.at[pos, self.rows(0)], self.passed.at[self.rows(0)], self.next
        )
        self.pass1 = self.wires.send(
            self.got.at[pos, self.rows(1)], self.passed.at[self.rows(1)], self.prev
        )

    def second(self):
        self.arriving = []
        after, before = turn(self.me, 1), turn(self.me, -1)
        for by, half, who, side in ((1, 1, self.next, 0), (-1, 0, self.prev, 1)):
            pos = turn(self.me, by)
            self.shared[by].wait_recv()
            mine = self.got.at[pos, self.rows(half)]
            add_into(mine, self.part.at[self.spot.c, pos, self.rows(half)], mine)
            self.arriving.append(self.wires.send(mine, self.near.at[side, self.rows(half)], who))
        for pos, half, who, side, arrived in (
            (after, 0, self.next, 0, self.pass0),
            (before, 1, self.prev, 1, self.pass1),
        ):
            arrived.wait_recv()
            mine = self.got.at[pos, self.rows(half)]
            add_into(
                mine,
                self.part.at[self.spot.c, pos, self.rows(half)],
                mine,
                self.passed.at[self.rows(half)],
            )
            self.arriving.append(self.wires.send(mine, self.near.at[side, self.rows(half)], who))

    def arrive(self):
        self.shared[0].wait_recv()
        for copy in self.arriving:
            copy.wait_recv()

    def close(self):
        self.wires.done(list(self.shared.values()) + [self.pass0, self.pass1] + self.arriving)

    def total(self, span):
        return (
            self.part[self.spot.c, self.me, span].astype(F32)
            + self.got[self.me, span].astype(F32)
            + self.near[0, span].astype(F32)
            + self.near[1, span].astype(F32)
        )


class LineScatter:
    def __init__(self, wires, spot, axis, at, passed, work, near):
        self.wires, self.at = wires, at
        self.me = spot.me(axis)
        self.next, self.prev = spot.along(axis, 1), spot.along(axis, -1)
        self.passed, self.work, self.near = passed, work, near

    def first(self):
        send, me = self.wires.send, self.me
        far, after, before = turn(me, 2), turn(me, 1), turn(me, -1)
        self.pass0 = send(self.at(far, 0), self.passed(0), self.next)
        self.pass1 = send(self.at(far, 1), self.passed(1), self.prev)
        self.arriving = [
            send(self.at(after, 1), self.near(0, 1), self.next),
            send(self.at(before, 0), self.near(1, 0), self.prev),
        ]

    def second(self):
        for by, half, who, side, arrived in (
            (1, 0, self.next, 0, self.pass0),
            (-1, 1, self.prev, 1, self.pass1),
        ):
            arrived.wait_recv()
            add_into(self.work(half), self.at(turn(self.me, by), half), self.passed(half))
            self.arriving.append(self.wires.send(self.work(half), self.near(side, half), who))

    def finish(self):
        for copy in self.arriving:
            copy.wait_recv()
        for half in (0, 1):
            mine = self.at(self.me, half)
            add_into(mine, mine, self.near(0, half), self.near(1, half))


def norm_scale(values):
    return lax.rsqrt(jnp.mean(values * values, axis=-1, keepdims=True) + EPSILON)


def norm_back(upstream, values, inverse, gain):
    scaled = upstream * gain
    inner = jnp.sum(scaled * values, axis=-1, keepdims=True)
    return scaled * inverse - values * inner * (inverse * inverse * inverse) / values.shape[-1]


def over_rows(start, size, step, chunk=16):
    def body(i, carry):
        step(pl.ds(pl.multiple_of(start + i * chunk, chunk), chunk))
        return carry

    lax.fori_loop(0, size // chunk, body, 0)


def fold(total, values):
    part = values[0:8]
    for first in range(8, values.shape[0], 8):
        part = part + values[first : first + 8]
    total[...] += part


SUBS = ((0, 96), (96, 96))


def dot(left, right, a, b):
    return lax.dot_general(left, right, (((a,), (b,)), ((), ())), preferred_element_type=F32)


def repeat(count, step):
    def body(i, carry):
        step(i)
        return carry

    lax.fori_loop(0, count, body, 0)


def whole(i, size):
    return pl.ds(pl.multiple_of(i * size, size), size)


def grid_of(rows, columns):
    return (
        lax.broadcasted_iota(jnp.int32, (rows, columns), 0),
        lax.broadcasted_iota(jnp.int32, (rows, columns), 1),
    )


def picks(rows, columns, chosen):
    return jnp.where(chosen(*grid_of(rows, columns)), 1.0, 0.0).astype(BF16)


def quad_order(unit):
    return (((unit >> 5) & 3) << 7) + ((unit >> 7) << 5) + (unit & 31)


def swap_halves(values):
    lane = lax.broadcasted_iota(jnp.int32, values.shape, 1)
    up = pltpu.roll(values, 80, 1)
    down = pltpu.roll(values, 48, 1)
    return jnp.where(lane < 48, up, down)


def around(spot, axes):
    return [spot.along(a, by) for a in axes for by in (1, -1)] + [spot.sibling]


def layer_kernel(
    tokens, gain_attn, gain_mlp, cot, w_query, w_key, w_value, w_out, w_gate, w_up, w_down, marks,
    normed_out, result_out, token_out, gains_out, att_out, out_out, gu_out, dn_out,
    normed, cots, second, part, got, passed, near, work, att_two, own_out, aq, ao, wq, wo,
    gu, gu_own, dn, d_gu, d_dn, own, grad_hidden, q, kv, prob, mix, cosine, sine,
    marks_two, gains, middle_all, back_all, total, grad_mix, grad_kv, far_kv,
    gu_in, dn_in, att_in, out_in, gain_c, gain_y, gain_x, gain_z,
    ready, send_sem, recv_sem,
):
    spot = Spot()
    wires = Wires(send_sem, recv_sem)
    x, y, z, c = spot.x, spot.y, spot.z, spot.c
    greet(
        around(spot, "xyz")
        + [spot.along(a, 2) for a in "xyz"]
        + [spot.partner]
        + [spot.in_quad(by)[1] for by in (1, 2, 3)]
    )

    def tell(which, devices):
        for who in devices:
            pl.semaphore_signal(ready.at[which], inc=1, device_id=who, device_id_type=MESH)

    def hear(which, count):
        pl.semaphore_wait(ready.at[which], count)

    def three(first):
        return lambda r, k: r + first == k

    columns = (
        dot(w_query[...], picks(192, 384, three(0)), 1, 0)
        + dot(w_key[...], picks(96, 384, three(192)), 1, 0)
        + dot(w_value[...], picks(96, 384, three(288)), 1, 0)
    )
    att_two[0] = columns.astype(BF16)
    own_out[0] = jnp.zeros((16, D), BF16)
    own_out[0, 0:12] = w_out[...]
    swaps = [
        wires.send(att_two.at[0], att_two.at[1], spot.partner),
        wires.send(own_out.at[0], own_out.at[1], spot.partner),
    ]
    dn_here = dn.at[whole(y * 4 + z, 32)]
    dn_kept = wires.move(w_down, dn_here)
    dn_side = [wires.send(w_down, dn_here, spot.along("z", by)) for by in (1, -1, 2)]
    marks_kept = wires.move(marks, marks_two.at[c])
    marks_got = wires.send(marks, marks_two.at[c], spot.sibling)
    for i, gain in enumerate((gain_attn, gain_mlp)):
        gains[i : i + 1, :] = jnp.concatenate([gain[j : j + 1, :] for j in range(12)], axis=1)

    def normalise(span):
        rows = tokens[span, :].astype(F32)
        own[span, :] = (rows * norm_scale(rows) * gains[0:1, :]).astype(BF16)

    over_rows(0, OWN, normalise)
    rows_y = [PairGather(wires, spot, "y", normed, own, s, n) for s, n in SUBS]
    for g in rows_y:
        g.start()

    order = picks(512, 512, lambda r, k: quad_order(r) == k)
    for shard, first in ((w_gate, 0), (w_up, 128)):
        moved = dot(shard[...], order, 1, 0).astype(BF16)
        for i in range(4):
            gu_own[i, :, first : first + 128] = moved[:, i * 128 : i * 128 + 128]
    gu_lanes = whole(y, 256)
    gu_here = gu.at[whole(z * 4 + spot.quad, 96), gu_lanes]
    gu_kept = wires.move(gu_own.at[spot.quad], gu_here)
    gu_swap = []
    for by in (1, 2, 3):
        other, who = spot.in_quad(by)
        gu_swap.append(wires.send(gu_own.at[other], gu_here, who))

    for copy in swaps:
        copy.wait_recv()
    slot = spot.low * 2 + spot.high
    pick = jnp.where(spot.high == c, 0, 1)
    aq_here, ao_here = aq.at[z, slot], ao.at[z, slot]
    att_kept = [wires.move(att_two.at[pick], aq_here), wires.move(own_out.at[pick], ao_here)]
    att_side = []
    for by in (1, -1, 2):
        who = spot.along("z", by)
        att_side.append(wires.send(att_two.at[pick], aq_here, who))
        att_side.append(wires.send(own_out.at[pick], ao_here, who))

    def trig(core):
        def step(i):
            span = whole(i, 128)
            row, lane = grid_of(128, 128)
            number = marks_two[core, pl.ds(spot.high * 6 + i, 1), :]
            ones = jnp.ones((128, 128), BF16)
            where = jnp.zeros((128, 128), F32)
            for digit, factor in ((number >> 5, 32.0), (number & 31, 1.0)):
                spread = jnp.where(row == lane, digit.astype(F32), 0.0).astype(BF16)
                where = where + factor * dot(spread, ones, 1, 0)
            grad_kv[core, span, 0:128] = where
            turns = jnp.where(lane < 48, lane, lane - 48).astype(F32) * (2.0 / HD)
            angle = where * jnp.exp(-math.log(ROPE_BASE) * turns)
            inside = lane < HD
            cosine[core, span, :] = jnp.where(inside, jnp.cos(angle), 0.0)
            wave = jnp.sin(angle)
            sine[core, span, :] = jnp.where(inside, jnp.where(lane < 48, -wave, wave), 0.0)

        repeat(6, step)

    marks_kept.wait()
    trig(c)
    for copy in att_kept:
        copy.wait()
    for copy in att_side:
        copy.wait_recv()

    def slot_of(pos):
        return (pos % 2) * 2 + pos // 2

    att_line = [
        RingGather(wires, spot, "x", lambda pos, h: aq.at[pl.ds(2 * h, 2), slot_of(pos)]),
        RingGather(wires, spot, "x", lambda pos, h: ao.at[pl.ds(2 * h, 2), slot_of(pos)]),
    ]
    for line in att_line:
        line.start()
    for g in rows_y:
        g.forward()
    marks_got.wait_recv()
    trig(1 - c)
    for line in att_line:
        line.forward()
    cot_x = [PairGather(wires, spot, "x", cots, cot, s, n) for s, n in SUBS]
    for g in cot_x:
        g.start()
    gu_kept.wait()
    for copy in gu_swap:
        copy.wait_recv()
    gu_block = gu.at[whole(z, 384), gu_lanes]
    gu_side = [wires.send(gu_block, gu_block, spot.along("y", by)) for by in (1, -1, 2)]
    dn_kept.wait()
    for copy in dn_side:
        copy.wait_recv()
    dn_line = RingGather(wires, spot, "y", lambda pos, h: dn.at[whole(pos * 2 + h, 64)])
    dn_line.start()
    for g in rows_y:
        g.far()
    for line in att_line:
        line.near()
        line.far()

    widen = picks(384, 512, lambda r, k: r + ((r * 683) >> 16) * 32 == k)

    def widen_rows(i):
        wq[i // 4, i % 4] = dot(aq[i // 4, i % 4], widen, 1, 0).astype(BF16)

    repeat(16, widen_rows)

    def out_row(r, k):
        unit = jnp.where(r < 128, r, r - 32)
        real = (r < 96) | ((r >= 128) & (r < 224))
        return real & (unit + ((unit * 5462) >> 16) * 4 == k)

    out_rows = picks(256, 256, out_row)
    wo[...] = dot(out_rows, ao[...].reshape(256, D), 1, 0).astype(BF16).reshape(4, 4, 16, D)

    for g in rows_y:
        g.finish()
    normed_kept = wires.move(normed, normed_out)

    def project(i):
        core, pos = i // 4, i % 4
        both = dot(normed[core, pos], wq[...].reshape(D, 512), 1, 0)
        span = whole(pos, OWN)
        cos, sin = cosine[core, span, :], sine[core, span, :]

        def turned(first):
            values = both[:, first : first + 128]
            return (values * cos + swap_halves(values) * sin).astype(BF16)

        q[core, span, 0:128] = turned(0)
        q[core, span, 128:256] = turned(128)
        after = pl.ds(pl.multiple_of(WIN + pos * OWN, 64), OWN)
        kv[core, after, 0:128] = turned(256)
        kv[core, after, 128:256] = both[:, 384:512].astype(BF16)

    repeat(8, project)
    kv_got = wires.send(kv.at[:, pl.ds(768, WIN)], kv.at[:, pl.ds(0, WIN)], spot.along("x", 2))

    for copy in gu_side:
        copy.wait_recv()
    gu_line = RingGather(
        wires, spot, "z", lambda pos, h: gu.at[whole(pos, 384), pl.ds(h * 512, 512)]
    )
    gu_line.start()

    scale = HD ** (-0.5)

    def attend(core, run, head):
        span = whole(run, WIN)
        lanes = whole(head, 128)
        window = pl.ds(pl.multiple_of(run * WIN, WIN), SEQ)
        scores = dot(q[core, span, lanes], kv[core, window, 0:128], 1, 1) * scale
        row, column = grid_of(WIN, SEQ)
        spot_of = spot.high * HALF + run * WIN + row[:, 0:1]
        begin = jnp.maximum((spot_of >> 9) << 9, spot_of - grad_kv[core, span, 0:1].astype(jnp.int32))
        begin = begin - (spot.high * HALF + run * WIN) + WIN
        allowed = (column >= begin) & (column <= row + WIN)
        scores = jnp.where(allowed, scores, MASKED)
        weights = jnp.exp(scores - jnp.max(scores, axis=-1, keepdims=True))
        share = weights / jnp.sum(weights, axis=-1, keepdims=True)
        low = share.astype(BF16)
        prob[core, run, head] = low
        values = dot(low, kv[core, window, 128:256], 1, 0)
        mix[core, span, lanes] = values.astype(BF16)

    repeat(8, lambda i: attend(i // 4, 1 + (i // 2) % 2, i % 2))
    for g in cot_x:
        g.forward()
    dn_line.forward()
    kv_got.wait_recv()
    repeat(4, lambda i: attend(i // 2, 0, i % 2))

    def project_out(core):
        def step(pos):
            rows = mix[core, whole(pos, OWN), :]
            part[core, pos] = dot(rows, wo[...].reshape(256, D), 1, 0).astype(BF16)

        repeat(4, step)

    sums_y = [PairScatter(wires, spot, "y", part, got, passed, near, s, n) for s, n in SUBS]
    project_out(1 - c)
    for by in (2, 1, -1, 0):
        for s in sums_y:
            s.share(by)
    project_out(c)
    for g in rows_y:
        g.close()
    normed_kept.wait()
    for s in sums_y:
        s.first()
    gu_line.forward()
    for g in cot_x:
        g.far()
    for s in sums_y:
        s.second()
    dn_line.near()
    dn_line.far()
    for g in cot_x:
        g.finish()

    def back_hidden(i):
        rows = cots[i // 2, pl.ds((i % 2) * 2, 2)].reshape(384, D)
        back = dot(rows, dn[...], 1, 1).astype(BF16)
        grad_hidden[i // 2, pl.ds((i % 2) * 2, 2)] = back.reshape(2, OWN, 512)

    repeat(4, back_hidden)
    rows_x = [PairGather(wires, spot, "x", second, own, s, n) for s, n in SUBS]

    def middle_rows(s):
        def use(span):
            middle = tokens[span, :].astype(F32) + s.total(span)
            middle_all[span, :] = middle
            own[span, :] = (middle * norm_scale(middle) * gains[1:2, :]).astype(BF16)

        return use

    for s, g in zip(sums_y, rows_x):
        s.arrive()
        over_rows(s.start_row, s.size, middle_rows(s))
        s.close()
        g.start()
        g.forward()
    gu_line.near()
    gu_line.far()
    rows_x[0].far()
    rows_x[0].finish()

    def feed(core, s):
        span = s.rows()
        size = 4 * s.size

        rows = second[core, :, span].reshape(size, D)
        both = dot(rows, gu[...], 1, 0)
        upstream = grad_hidden[core, :, span].reshape(size, 512).astype(F32)
        for i in range(4):
            gate = both[:, i * 256 : i * 256 + 128]
            upward = both[:, i * 256 + 128 : i * 256 + 256]
            sent = upstream[:, i * 128 : i * 128 + 128]
            sigmoid = jax.nn.sigmoid(gate)
            silu = gate * sigmoid
            slope = sigmoid * (1.0 + gate * (1.0 - sigmoid))
            low = (silu * upward).astype(BF16)
            work[core, :, span, 1024 + i * 128 : 1152 + i * 128] = low.reshape(4, s.size, 128)
            low = (sent * upward * slope).astype(BF16)
            work[core, :, span, i * 256 : i * 256 + 128] = low.reshape(4, s.size, 128)
            low = (sent * silu).astype(BF16)
            work[core, :, span, i * 256 + 128 : i * 256 + 256] = low.reshape(4, s.size, 128)
        back = dot(work[core, :, span, 0:1024].reshape(size, 1024), gu[...], 1, 1)
        part[core, :, span] = back.astype(BF16).reshape(4, s.size, D)

    early = list(wires.sent)
    sums_x = [PairScatter(wires, spot, "x", part, got, passed, near, s, n) for s, n in SUBS]
    feed(1 - c, sums_x[0])
    for by in (2, 1, -1, 0):
        sums_x[0].share(by)
    rows_x[1].far()
    feed(c, sums_x[0])
    sums_x[0].first()
    rows_x[1].finish()
    feed(1 - c, sums_x[1])
    for by in (2, 1, -1, 0):
        sums_x[1].share(by)
    sums_x[0].second()
    feed(c, sums_x[1])
    sums_x[1].first()

    def grad_gate_up(i):
        lanes = whole(i, 256)
        rows = second[:, :, :, lanes].reshape(8 * OWN, 256)
        d_gu[lanes, :] = dot(rows, work[:, :, :, 0:1024].reshape(8 * OWN, 1024), 0, 0).astype(BF16)

    def grad_down(i):
        lanes = pl.ds(pl.multiple_of(1024 + i * 256, 256), 256)
        rows = work[:, :, :, lanes].reshape(8 * OWN, 256)
        d_dn[whole(i, 256), :] = dot(rows, cots[...].reshape(8 * OWN, D), 0, 0).astype(BF16)

    def down(i):
        rows = work[i // 2, pl.ds((i % 2) * 2, 2), :, 1024:D].reshape(384, 512)
        second[i // 2, pl.ds((i % 2) * 2, 2)] = (
            dot(rows, dn[...], 1, 0).astype(BF16).reshape(2, OWN, D)
        )

    total[...] = jnp.zeros_like(total)
    grads_y = [PairGather(wires, spot, "y", normed, own, s, n) for s, n in SUBS]

    def back_rows(s):
        def use(span):
            grad = s.total(span)
            rows = middle_all[span, :]
            inverse = norm_scale(rows)
            back = cot[span, :].astype(F32) + norm_back(grad, rows, inverse, gains[1:2, :])
            back_all[span, :] = back
            own[span, :] = back.astype(BF16)
            fold(total, grad * rows * inverse)

        return use

    wires.done(early)
    for g in rows_x:
        g.close()
    tell(0, [spot.along("z", 1), spot.along("z", -1)])
    repeat(2, grad_gate_up)
    sums_x[1].second()
    sums_x[0].arrive()
    over_rows(sums_x[0].start_row, sums_x[0].size, back_rows(sums_x[0]))
    sums_x[0].close()
    grads_y[0].start()
    repeat(2, lambda i: grad_gate_up(2 + i))
    grads_y[0].forward()
    sums_x[1].arrive()
    over_rows(sums_x[1].start_row, sums_x[1].size, back_rows(sums_x[1]))
    sums_x[1].close()
    grads_y[1].start()
    repeat(2, lambda i: grad_gate_up(4 + i))
    hear(0, 2)
    gu_sum = LineScatter(
        wires, spot, "z",
        lambda pos, h: d_gu.at[whole(pos * 2 + h, 192)],
        lambda h: gu.at[pl.ds(h * 192, 192)],
        lambda h: gu.at[pl.ds(384 + h * 192, 192)],
        lambda side, h: gu.at[pl.ds(768 + side * 384 + h * 192, 192)],
    )
    gu_sum.first()
    grads_y[1].forward()
    grads_y[0].far()
    repeat(2, grad_down)
    grads_y[1].far()
    repeat(4, down)
    tell(1, around(spot, "xy"))
    gain_c[c, 1:2] = jnp.sum(total[...], axis=0, keepdims=True)
    total[...] = jnp.zeros_like(total)
    again = wires.move(normed_out, cots)
    for g in grads_y:
        g.finish()

    def mix_back(i):
        span = whole(i % 4, OWN)
        rows = dot(normed[i // 4, i % 4], wo[...].reshape(256, D), 1, 1)
        grad_mix[i // 4, span, :] = rows.astype(BF16)

    repeat(8, mix_back)
    hear(1, 5)
    sums_m = [
        PairScatter(
            wires, spot, "x", second, work.at[0], work.at[1, 0], work.at[1, pl.ds(1, 2)], s, n
        )
        for s, n in SUBS
    ]
    for by in (2, 1, -1, 0):
        for s in sums_m:
            s.share(by)
    dn_sum = LineScatter(
        wires, spot, "y",
        lambda pos, h: d_dn.at[whole(pos * 2 + h, 64)],
        lambda h: dn.at[pl.ds(h * 64, 64)],
        lambda h: dn.at[pl.ds(128 + h * 64, 64)],
        lambda side, h: dn.at[pl.ds(256 + side * 128 + h * 64, 64)],
    )
    dn_sum.first()
    grad_kv[...] = jnp.zeros_like(grad_kv)

    def attend_back(core, run, head):
        span = whole(run, WIN)
        lanes = whole(head, 128)
        window = pl.ds(pl.multiple_of(run * WIN, WIN), SEQ)
        low = prob[core, run, head]
        share = low.astype(F32)
        mixed = grad_mix[core, span, lanes]
        asked = q[core, span, lanes]
        grad = dot(mixed, kv[core, window, 128:256], 1, 1)
        inner = jnp.sum(share * grad, axis=-1, keepdims=True)
        scored = (share * (grad - inner)).astype(BF16)
        grad_kv[core, window, 0:128] += dot(scored, asked, 0, 0) * scale
        grad_kv[core, window, 128:256] += dot(low, mixed, 0, 0)
        grad_q = dot(scored, kv[core, window, 0:128], 1, 0) * scale
        cos, sin = cosine[core, span, :], sine[core, span, :]
        q[core, span, lanes] = (grad_q * cos - swap_halves(grad_q) * sin).astype(BF16)

    repeat(4, lambda i: attend_back(i // 2, 0, i % 2))
    own_far = att_far = grad_mix.at[:, pl.ds(0, WIN)]
    for core in (0, 1):
        own_far[core] = grad_kv[core, 0:WIN, :].astype(BF16)
    far_got = wires.send(att_far, far_kv, spot.along("x", 2))
    repeat(4, lambda i: attend_back(i // 2, 1, i % 2))
    for s in sums_m:
        s.first()
    gu_sum.second()
    dn_sum.second()
    repeat(4, lambda i: attend_back(i // 2, 2, i % 2))
    for s in sums_m:
        s.second()
    far_got.wait_recv()
    for core in (0, 1):
        grad_kv[core, 768:1024, :] += far_kv[core].astype(F32)

    def turn_back(i):
        core, pos = i // 4, i % 4
        after = pl.ds(pl.multiple_of(WIN + pos * OWN, 64), OWN)
        span = whole(pos, OWN)
        grad = grad_kv[core, after, 0:128]
        cos, sin = cosine[core, span, :], sine[core, span, :]
        kv[core, after, 0:128] = (grad * cos - swap_halves(grad) * sin).astype(BF16)
        kv[core, after, 128:256] = grad_kv[core, after, 128:256].astype(BF16)

    repeat(8, turn_back)


    def normed_back(core):
        def step(pos):
            span = whole(pos, OWN)
            after = pl.ds(pl.multiple_of(WIN + pos * OWN, 64), OWN)
            rows = jnp.concatenate([q[core, span, :], kv[core, after, :]], axis=1)
            part[core, pos] = dot(rows, wq[...].reshape(D, 512), 1, 1).astype(BF16)

        repeat(4, step)

    sums_n = [PairScatter(wires, spot, "y", part, got, passed, near, s, n) for s, n in SUBS]
    normed_back(1 - c)
    for by in (2, 1, -1, 0):
        for s in sums_n:
            s.share(by)
    normed_back(c)
    for s in sums_n:
        s.first()

    def out_rows_back(r, k):
        unit = jnp.where(k < 128, k, k - 32)
        real = (k < 96) | ((k >= 128) & (k < 224))
        return real & (unit + ((unit * 5462) >> 16) * 4 == r)

    grad_out = dot(mix[...].reshape(8 * OWN, 256), normed[...].reshape(8 * OWN, D), 0, 0)
    grad_out = dot(picks(256, 256, out_rows_back), grad_out.astype(BF16), 1, 0)
    wo[...] = grad_out.astype(BF16).reshape(4, 4, 16, D)
    again.wait()
    narrow = picks(512, 384, lambda r, k: k + ((k * 683) >> 16) * 32 == r)

    def grad_columns(i):
        rows = cots[:, :, :, whole(i, 384)].reshape(8 * OWN, 384)
        grad = dot(rows, q[...].reshape(8 * OWN, 256), 0, 0).astype(BF16)
        grad = dot(grad, narrow[0:256], 1, 0)
        keyed = kv[:, pl.ds(WIN, HALF), :].reshape(8 * OWN, 256)
        other = dot(rows, keyed, 0, 0).astype(BF16)
        grad = (grad + dot(other, narrow[256:512], 1, 0)).astype(BF16)
        wq[i, :, :, 0:384] = grad.reshape(4, 96, 384)

    repeat(4, grad_columns)
    att_sum = [
        LineScatter(
            wires, spot, "x",
            lambda pos, h: wq.at[pl.ds(2 * h, 2), slot_of(pos), :, pl.ds(0, 384)],
            lambda h: aq.at[0, pl.ds(2 * h, 2)],
            lambda h: aq.at[1, pl.ds(2 * h, 2)],
            lambda side, h: aq.at[2 + side, pl.ds(2 * h, 2)],
        ),
        LineScatter(
            wires, spot, "x",
            lambda pos, h: wo.at[pl.ds(2 * h, 2), slot_of(pos)],
            lambda h: ao.at[0, pl.ds(2 * h, 2)],
            lambda h: ao.at[1, pl.ds(2 * h, 2)],
            lambda side, h: ao.at[2 + side, pl.ds(2 * h, 2)],
        ),
    ]
    for line in att_sum:
        line.first()
    for s in sums_n:
        s.second()

    gu_sum.finish()
    gu_got = [
        wires.send(d_gu.at[whole(z, 384), whole(turn(y, by), 256)], gu_in.at[y], spot.along("y", by))
        for by in (1, -1, 2)
    ]
    dn_sum.finish()
    dn_got = [
        wires.send(d_dn.at[whole(y * 4 + turn(z, by), 32)], dn_in.at[z], spot.along("z", by))
        for by in (1, -1, 2)
    ]

    def result_rows(s):
        def use(span):
            second[c, x, span] = (middle_all[span, :] + s.total(span)).astype(BF16)

        return use

    for s in sums_m:
        s.arrive()
        over_rows(s.start_row, s.size, result_rows(s))
    result_kept = wires.move(second.at[c, x], result_out)
    for line in att_sum:
        line.second()

    def token_rows(s):
        def use(span):
            grad = s.total(span)
            rows = tokens[span, :].astype(F32)
            inverse = norm_scale(rows)
            out = back_all[span, :] + norm_back(grad, rows, inverse, gains[0:1, :])
            part[c, y, span] = out.astype(BF16)
            fold(total, grad * rows * inverse)

        return use

    for s in sums_n:
        s.arrive()
        over_rows(s.start_row, s.size, token_rows(s))
    token_kept = wires.move(part.at[c, y], token_out)
    gain_c[c, 0:1] = jnp.sum(total[...], axis=0, keepdims=True)
    gain_got = [wires.send(gain_c.at[c], gain_c.at[c], spot.sibling)]

    for copy in gu_got:
        copy.wait_recv()
    mine = d_gu.at[whole(z, 384), whole(y, 256)]
    add_into(mine, mine, *[gu_in.at[turn(y, by)] for by in (1, -1, 2)])
    gu_done = []
    for by in (1, 2, 3):
        other, who = spot.in_quad(by)
        gu_done.append(
            wires.send(
                d_gu.at[whole(z * 4 + other, 96), whole(y, 256)], gu_own.at[spot.quad], who
            )
        )
    for line in att_sum:
        line.finish()
    slot_me = slot_of(x)
    att_got = []
    for by in (1, -1, 2):
        far = turn(z, by)
        who = spot.along("z", by)
        att_got.append(
            wires.send(wq.at[far, slot_me, :, pl.ds(0, 384)], att_in.at[z], who)
        )
        att_got.append(wires.send(wo.at[far, slot_me], out_in.at[z], who))

    held = gain_c
    for axis, into in (("y", gain_y), ("x", gain_x), ("z", gain_z), (None, None)):
        for copy in gain_got:
            copy.wait_recv()
        summed = held[0]
        for i in range(1, held.shape[0]):
            summed = summed + held[i]
        if into is None:
            gains_out[...] = summed
            break
        me = spot.me(axis)
        into[me] = summed
        gain_got = [
            wires.send(into.at[me], into.at[me], spot.along(axis, by)) for by in (1, -1, 2)
        ]
        held = into
        if axis == "y":
            for copy in dn_got:
                copy.wait_recv()
            add_into(
                dn_out,
                d_dn.at[whole(y * 4 + z, 32)],
                *[dn_in.at[turn(z, by)] for by in (1, -1, 2)],
            )
        if axis == "x":
            for copy in att_got:
                copy.wait_recv()
            others = [turn(z, by) for by in (1, -1, 2)]
            add_into(
                att_two.at[0],
                wq.at[z, slot_me, :, pl.ds(0, 384)],
                *[att_in.at[far] for far in others],
            )
            add_into(own_out.at[0], wo.at[z, slot_me], *[out_in.at[far] for far in others])
            swaps = [
                wires.send(att_two.at[0], att_two.at[1], spot.partner),
                wires.send(own_out.at[0], own_out.at[1], spot.partner),
            ]
    kept_rows = d_gu.at[whole(z * 4 + spot.quad, 96), whole(y, 256)]
    gu_out[spot.quad] = kept_rows[...]
    for copy in gu_done:
        copy.wait_recv()
    for by in (1, 2, 3):
        other = turn(spot.quad, by)
        gu_out[other] = gu_own[other]
    for copy in swaps:
        copy.wait_recv()
    att_out[...] = att_two[pick]
    out_out[...] = own_out[pick]
    result_kept.wait()
    token_kept.wait()
    wires.close()


def finish_kernel(
    result, token, gains, att, out, gu, dn,
    result_out, token_out, attn_out, mlp_out, query_out, key_out, value_out, out_out,
    gate_out, up_out, dn_out,
):
    result_out[...] = result[...]
    token_out[...] = token[...]
    for i, into in enumerate((attn_out, mlp_out)):
        for j in range(12):
            into[j : j + 1, :] = gains[i : i + 1, j * 128 : j * 128 + 128]
    rows = att[...]

    def three(first):
        return lambda r, k: r == k + first

    query_out[...] = dot(rows, picks(384, 192, three(0)), 1, 0)
    key_out[...] = dot(rows, picks(384, 96, three(192)), 1, 0)
    value_out[...] = dot(rows, picks(384, 96, three(288)), 1, 0)
    out_out[...] = out[0:12, :].astype(F32)
    order = picks(512, 512, lambda r, k: quad_order(k) == r)
    for first, into in ((0, gate_out), (128, up_out)):
        moved = jnp.concatenate([gu[i, :, first : first + 128] for i in range(4)], axis=1)
        into[...] = dot(moved, order, 1, 0)
    dn_out[...] = dn[...]


def layer_call(
    tokens, gain_attn, gain_mlp, cot, w_query, w_key, w_value, w_out, w_gate, w_up, w_down, marks
):
    sems = 288
    shape = jax.ShapeDtypeStruct
    outs = (
        (shape((2, 4, OWN, D), BF16), ANY),
        (shape((OWN, D), BF16), ANY),
        (shape((OWN, D), BF16), ANY),
        (shape((2, D), F32), VMEM),
        (shape((96, 384), BF16), VMEM),
        (shape((16, D), BF16), VMEM),
        (shape((4, 96, 256), BF16), VMEM),
        (shape((32, D), F32), VMEM),
    )
    scratch = [
        ((2, 4, OWN, D), BF16),
        ((2, 4, OWN, D), BF16),
        ((2, 4, OWN, D), BF16),
        ((2, 4, OWN, D), BF16),
        ((4, OWN, D), BF16),
        ((OWN, D), BF16),
        ((2, OWN, D), BF16),
        ((2, 4, OWN, D), BF16),
        ((2, 96, 384), BF16),
        ((2, 16, D), BF16),
        ((4, 4, 96, 384), BF16),
        ((4, 4, 16, D), BF16),
        ((4, 4, 96, 512), BF16),
        ((4, 4, 16, D), BF16),
        ((D, 1024), BF16),
        ((4, 96, 256), BF16),
        ((512, D), BF16),
        ((D, 1024), BF16),
        ((512, D), BF16),
        ((OWN, D), BF16),
        ((2, 4, OWN, 512), BF16),
        ((2, HALF, 256), BF16),
        ((2, HALF + WIN, 256), BF16),
        ((2, 3, 2, WIN, SEQ), BF16),
        ((2, HALF, 256), BF16),
        ((2, HALF, 128), F32),
        ((2, HALF, 128), F32),
        ((2, 12, 128), jnp.int32),
        ((2, D), F32),
        ((OWN, D), F32),
        ((OWN, D), F32),
        ((8, D), F32),
        ((2, HALF, 256), BF16),
        ((2, HALF + WIN, 256), F32),
        ((2, WIN, 256), BF16),
        ((4, 384, 256), BF16),
        ((4, 32, D), BF16),
        ((4, 96, 384), BF16),
        ((4, 16, D), BF16),
        ((2, 2, D), F32),
        ((4, 2, D), F32),
        ((4, 2, D), F32),
        ((4, 2, D), F32),
    ]
    outs_raw = pl.pallas_call(
        layer_kernel,
        out_shape=tuple(o[0] for o in outs),
        in_specs=[VMEM] * 12,
        out_specs=[o[1] for o in outs],
        scratch_shapes=[pltpu.VMEM(*s) for s in scratch]
        + [
            pltpu.SemaphoreType.REGULAR((2,)),
            pltpu.SemaphoreType.DMA((sems,)),
            pltpu.SemaphoreType.DMA((sems,)),
        ],
        compiler_params=pltpu.CompilerParams(
            collective_id=1, has_side_effects=True, vmem_limit_bytes=64 << 20
        ),
        name="layer",
    )(tokens, gain_attn, gain_mlp, cot, w_query, w_key, w_value, w_out, w_gate, w_up, w_down, marks)
    finals = (
        shape((OWN, D), BF16),
        shape((OWN, D), BF16),
        shape((12, 128), F32),
        shape((12, 128), F32),
        shape((96, 192), F32),
        shape((96, 96), F32),
        shape((96, 96), F32),
        shape((12, D), F32),
        shape((96, 512), F32),
        shape((96, 512), F32),
        shape((32, D), F32),
    )
    return pl.pallas_call(
        finish_kernel,
        out_shape=finals,
        in_specs=[VMEM] * 7,
        out_specs=[VMEM] * 11,
        name="finish",
    )(*outs_raw[1:])


def shards(
    tokens,
    gain_attn,
    gain_mlp,
    w_query,
    w_key,
    w_value,
    w_out,
    w_gate,
    w_up,
    w_down,
    segments,
    positions,
    cotangent,
):
    del segments
    done = layer_call(
        tokens,
        gain_attn.reshape(12, 128),
        gain_mlp.reshape(12, 128),
        cotangent,
        w_query,
        w_key,
        w_value,
        w_out,
        w_gate,
        w_up,
        w_down,
        positions.reshape(12, 128),
    )
    return (*done[:2], done[2].reshape(D), done[3].reshape(D), *done[4:])


def solution(mesh):
    placed = (
        P(("dp", "tensor"), None),
        P(),
        P(),
        P("dp", "tensor"),
        P("dp", "tensor"),
        P("dp", "tensor"),
        P(("tensor", "dp"), None),
        P("dp", "tensor"),
        P("dp", "tensor"),
        P(("tensor", "dp"), None),
        P("dp"),
        P("dp"),
        P(("dp", "tensor"), None),
    )
    return jax.shard_map(
        shards,
        mesh=mesh,
        in_specs=placed,
        out_specs=(
            P(("dp", "tensor"), None),
            P(("dp", "tensor"), None),
            P(),
            P(),
            P("dp", "tensor"),
            P("dp", "tensor"),
            P("dp", "tensor"),
            P(("tensor", "dp"), None),
            P("dp", "tensor"),
            P("dp", "tensor"),
            P(("tensor", "dp"), None),
        ),
        check_vma=False,
    )
```

profile of v0, /device:TPU:1, one launch (start us, length us, event | category | flops | bytes accessed | tf_op | source)
XLA Modules:
  0.0 226.9 jit_solution(15883997391934407052)
XLA Ops:
  0.6 223.1 %layer.1 = (bf16[2,4,192,1536]{3,2,1,0:T(8,128)(2,1)}, bf16[192,1536]{1,0:T(8,128)(2,1)}, bf16[192,1536]{1,0:T(8,128)(2,1)}, f32[2,1536]{1,0:T(2,128)}, bf16[96,...) custom-call(bf16[192,1536]{1,0:T(8,128)(2,1)} %tokens.1, ...), custom_call_target="tpu_custom_call" | custom-call | tf_op jit(solution)/shard_map/layer/pallas_call | solution.py:1103
  223.8 3.1 %finish.1 = (bf16[192,1536]{1,0:T(8,128)(2,1)}, bf16[192,1536]{1,0:T(8,128)(2,1)}, f32[12,128]{1,0:T(8,128)}, f32[12,128]{1,0:T(8,128)}, f32[96,192]{1,0:T(8,128...) custom-call(bf16[192,1536]{1,0:T(8,128)(2,1)} %get-tuple-element.29., ...), custom_call_target="tpu_custom_call" | custom-call | tf_op jit(solution)/shard_map/finish/pallas_call | solution.py:1132
where the time goes:
time: 227 us
  Pallas kernels  226 us (100%)
    pallas_call x1, Pallas kernels, layer_call(): pl.pallas_call(layer_kernel, out_shape=tuple((o[0] for o in outs)), in_sp...  223 us

commit v1 on v0

v1 whole, which is shorter than its diff:
```python
import functools
import math

import jax
import jax.numpy as jnp
from jax import lax
from jax.experimental import pallas as pl
from jax.experimental.pallas import tpu as pltpu
from jax.sharding import PartitionSpec as P

HD = 96
SEQ = 512
D = 1536
OWN = 192
HALF = 768
WIN = 256

EPSILON = 1e-05
ROPE_BASE = 100000.0
MASKED = -1e30
MESH = pl.DeviceIdType.MESH
ANY = pl.BlockSpec(memory_space=pl.ANY)
VMEM = pl.BlockSpec(memory_space=pltpu.VMEM)
BF16 = jnp.bfloat16
F32 = jnp.float32


def place():
    dp = lax.axis_index("dp")
    tensor = lax.axis_index("tensor")
    return (tensor // 4) * 2 + (dp // 2) % 2, tensor % 4, dp // 4, dp % 2


def device(x, y, z, c):
    return (z * 4 + (x % 2) * 2 + c, (x // 2) * 4 + y)


def turn(pos, by):
    return (pos + by + 4) % 4


class Spot:
    def __init__(self):
        x, y, z, c = place()
        self.x, self.y, self.z, self.c = x, y, z, c
        self.high, self.low = x // 2, x % 2
        self.quad = self.low * 2 + c
        self.sibling = device(x, y, z, 1 - c)
        self.partner = device(turn(x, 2), y, z, 1 - c)

    def along(self, axis, by):
        x, y, z, c = self.x, self.y, self.z, self.c
        if axis == "x":
            return device(turn(x, by), y, z, c)
        if axis == "y":
            return device(x, turn(y, by), z, c)
        return device(x, y, turn(z, by), c)

    def me(self, axis):
        return {"x": self.x, "y": self.y, "z": self.z}[axis]

    def in_quad(self, by):
        other = turn(self.quad, by)
        return other, device(self.high * 2 + other // 2, self.y, self.z, other % 2)


def greet(devices):
    for who in devices:
        pl.semaphore_signal(
            pltpu.get_barrier_semaphore(), inc=1, device_id=who, device_id_type=MESH
        )


def greeted(devices):
    pl.semaphore_wait(pltpu.get_barrier_semaphore(), len(devices))


class Wires:
    def __init__(self, send_sem, recv_sem):
        self.send_sem, self.recv_sem = send_sem, recv_sem
        self.free = list(range(send_sem.shape[0]))
        self.count = 0
        self.sent = []

    def again(self):
        self.count = 0

    def take(self):
        held = min(self.free)
        self.free.remove(held)
        return held

    def send(self, src, dst, who):
        held = self.take()
        assert self.count < self.recv_sem.shape[0]
        copy = pltpu.make_async_remote_copy(
            src_ref=src,
            dst_ref=dst,
            send_sem=self.send_sem.at[held],
            recv_sem=self.recv_sem.at[self.count],
            device_id=who,
            device_id_type=MESH,
        )
        self.count += 1
        copy.start()
        self.sent.append((copy, held))
        return copy

    def move(self, src, dst):
        held = self.take()
        copy = pltpu.make_async_copy(src, dst, self.send_sem.at[held])
        copy.start()
        return Moved(self, copy, held)

    def done(self, copies):
        kept = []
        for copy, held in self.sent:
            if any(copy is other for other in copies):
                copy.wait_send()
                self.free.append(held)
            else:
                kept.append((copy, held))
        self.sent = kept

    def started(self):
        return [copy for copy, _ in self.sent]

    def close(self):
        self.done(self.started())


class Moved:
    def __init__(self, wires, copy, held):
        self.wires, self.copy, self.held = wires, copy, held

    def wait(self):
        self.copy.wait()
        self.wires.free.append(self.held)


def add_into(dst, *srcs, chunk=16):
    rows = dst.shape[-2]
    chunk = min(chunk, rows)

    def step(i, carry):
        span = pl.ds(pl.multiple_of(i * chunk, chunk), chunk)
        total = srcs[0][..., span, :].astype(F32)
        for src in srcs[1:]:
            total = total + src[..., span, :].astype(F32)
        dst[..., span, :] = total.astype(dst.dtype)
        return carry

    lax.fori_loop(0, rows // chunk, step, 0)


class RingGather:
    def __init__(self, wires, spot, axis, at):
        self.wires, self.at = wires, at
        self.me = spot.me(axis)
        self.next, self.prev = spot.along(axis, 1), spot.along(axis, -1)

    def start(self, own=None):
        own = own or (lambda half: self.at(self.me, half))
        send, at, me = self.wires.send, self.at, self.me
        self.right0 = send(own(0), at(me, 0), self.next)
        self.left1 = send(own(1), at(me, 1), self.prev)
        self.right1 = send(own(1), at(me, 1), self.next)
        self.left0 = send(own(0), at(me, 0), self.prev)

    def forward(self):
        send, at, me = self.wires.send, self.at, self.me
        self.right0.wait_recv()
        before = at(turn(me, -1), 0)
        self.pass0 = send(before, before, self.next)
        self.left1.wait_recv()
        after = at(turn(me, 1), 1)
        self.pass1 = send(after, after, self.prev)

    def near(self):
        self.right1.wait_recv()
        self.left0.wait_recv()

    def far(self):
        self.pass0.wait_recv()
        self.pass1.wait_recv()

    def close(self):
        near = [self.right0, self.left1, self.right1, self.left0]
        self.wires.done(near + [self.pass0, self.pass1])


class PairGather:
    def __init__(self, wires, spot, axis, out, own, start, size):
        self.wires, self.spot, self.out, self.own = wires, spot, out, own
        self.rows = pl.ds(start, size)
        cut = size // 2

        def half_rows(half):
            return pl.ds(start + half * cut, cut)

        self.half_rows = half_rows
        self.ring = RingGather(
            wires, spot, axis, lambda pos, half: out.at[spot.c, pos, half_rows(half)]
        )
        self.me = spot.me(axis)

    def share(self, pos):
        block = self.out.at[self.spot.c, pos, self.rows]
        return self.wires.send(block, block, self.spot.sibling)

    def start(self):
        self.ring.start(lambda half: self.own.at[self.half_rows(half)])
        mine = self.own.at[self.rows]
        place_of = self.out.at[self.spot.c, self.me, self.rows]
        self.shared = [self.wires.send(mine, place_of, self.spot.sibling)]
        self.kept = self.wires.move(mine, place_of)

    def forward(self):
        self.ring.forward()

    def near(self):
        self.ring.near()
        self.shared.append(self.share(turn(self.me, -1)))
        self.shared.append(self.share(turn(self.me, 1)))

    def far(self):
        self.ring.far()
        self.shared.append(self.share(turn(self.me, 2)))

    def finish(self):
        for copy in self.shared:
            copy.wait_recv()
        self.kept.wait()

    def close(self):
        self.ring.close()
        self.wires.done(self.shared)


class PairScatter:
    def __init__(self, wires, spot, axis, part, got, passed, near, start, size):
        self.wires, self.spot = wires, spot
        self.me = spot.me(axis)
        self.next, self.prev = spot.along(axis, 1), spot.along(axis, -1)
        self.part, self.got, self.passed, self.near = part, got, passed, near
        self.start_row, self.size, self.cut = start, size, size // 2

    def rows(self, half=None):
        if half is None:
            return pl.ds(self.start_row, self.size)
        return pl.ds(self.start_row + half * self.cut, self.cut)

    def share(self):
        self.shared = self.wires.send(
            self.part.at[1 - self.spot.c, :, self.rows()],
            self.got.at[:, self.rows()],
            self.spot.sibling,
        )

    def first(self):
        self.shared.wait_recv()
        pos = turn(self.me, 2)
        mine = self.got.at[pos, self.rows()]
        add_into(mine, self.part.at[self.spot.c, pos, self.rows()], mine)
        self.pass0 = self.wires.send(
            self.got.at[pos, self.rows(0)], self.passed.at[self.rows(0)], self.next
        )
        self.pass1 = self.wires.send(
            self.got.at[pos, self.rows(1)], self.passed.at[self.rows(1)], self.prev
        )

    def direct(self):
        self.arriving = []
        for by, half, who, side in ((1, 1, self.next, 0), (-1, 0, self.prev, 1)):
            pos = turn(self.me, by)
            mine = self.got.at[pos, self.rows(half)]
            add_into(mine, self.part.at[self.spot.c, pos, self.rows(half)], mine)
            self.arriving.append(self.wires.send(mine, self.near.at[side, self.rows(half)], who))

    def through(self):
        after, before = turn(self.me, 1), turn(self.me, -1)
        for pos, half, who, side, arrived in (
            (after, 0, self.next, 0, self.pass0),
            (before, 1, self.prev, 1, self.pass1),
        ):
            arrived.wait_recv()
            mine = self.got.at[pos, self.rows(half)]
            add_into(
                mine,
                self.part.at[self.spot.c, pos, self.rows(half)],
                mine,
                self.passed.at[self.rows(half)],
            )
            self.arriving.append(self.wires.send(mine, self.near.at[side, self.rows(half)], who))

    def arrive(self):
        for copy in self.arriving:
            copy.wait_recv()

    def close(self):
        self.wires.done([self.shared, self.pass0, self.pass1] + self.arriving)

    def total(self, span):
        return (
            self.part[self.spot.c, self.me, span].astype(F32)
            + self.got[self.me, span].astype(F32)
            + self.near[0, span].astype(F32)
            + self.near[1, span].astype(F32)
        )


class LineScatter:
    def __init__(self, wires, spot, axis, at, passed, work, near):
        self.wires, self.at = wires, at
        self.me = spot.me(axis)
        self.next, self.prev = spot.along(axis, 1), spot.along(axis, -1)
        self.passed, self.work, self.near = passed, work, near

    def first(self):
        send, me = self.wires.send, self.me
        far, after, before = turn(me, 2), turn(me, 1), turn(me, -1)
        self.pass0 = send(self.at(far, 0), self.passed(0), self.next)
        self.pass1 = send(self.at(far, 1), self.passed(1), self.prev)
        self.arriving = [
            send(self.at(after, 1), self.near(0, 1), self.next),
            send(self.at(before, 0), self.near(1, 0), self.prev),
        ]

    def second(self):
        for by, half, who, side, arrived in (
            (1, 0, self.next, 0, self.pass0),
            (-1, 1, self.prev, 1, self.pass1),
        ):
            arrived.wait_recv()
            add_into(self.work(half), self.at(turn(self.me, by), half), self.passed(half))
            self.arriving.append(self.wires.send(self.work(half), self.near(side, half), who))

    def finish(self):
        for copy in self.arriving:
            copy.wait_recv()
        for half in (0, 1):
            mine = self.at(self.me, half)
            add_into(mine, mine, self.near(0, half), self.near(1, half))


def norm_scale(values):
    return lax.rsqrt(jnp.mean(values * values, axis=-1, keepdims=True) + EPSILON)


def norm_back(upstream, values, inverse, gain):
    scaled = upstream * gain
    inner = jnp.sum(scaled * values, axis=-1, keepdims=True)
    return scaled * inverse - values * inner * (inverse * inverse * inverse) / values.shape[-1]


def over_rows(start, size, step, chunk=16):
    def body(i, carry):
        step(pl.ds(pl.multiple_of(start + i * chunk, chunk), chunk))
        return carry

    lax.fori_loop(0, size // chunk, body, 0)


def fold(total, values):
    part = values[0:8]
    for first in range(8, values.shape[0], 8):
        part = part + values[first : first + 8]
    total[...] += part


TWO = ((0, 96), (96, 96))
THREE = ((0, 64), (64, 64), (128, 64))


def dot(left, right, a, b):
    return lax.dot_general(left, right, (((a,), (b,)), ((), ())), preferred_element_type=F32)


def repeat(count, step):
    def body(i, carry):
        step(i)
        return carry

    lax.fori_loop(0, count, body, 0)


def whole(i, size):
    return pl.ds(pl.multiple_of(i * size, size), size)


def grid_of(rows, columns):
    return (
        lax.broadcasted_iota(jnp.int32, (rows, columns), 0),
        lax.broadcasted_iota(jnp.int32, (rows, columns), 1),
    )


def picks(rows, columns, chosen):
    return jnp.where(chosen(*grid_of(rows, columns)), 1.0, 0.0).astype(BF16)


def quad_order(unit):
    return (((unit >> 5) & 3) << 7) + ((unit >> 7) << 5) + (unit & 31)


def swap_halves(values):
    lane = lax.broadcasted_iota(jnp.int32, values.shape, 1)
    up = pltpu.roll(values, 80, 1)
    down = pltpu.roll(values, 48, 1)
    return jnp.where(lane < 48, up, down)


def around(spot, axes):
    return [spot.along(a, by) for a in axes for by in (1, -1)] + [spot.sibling]


def layer_kernel(
    tokens, gain_attn, gain_mlp, cot, w_query, w_key, w_value, w_out, w_gate, w_up, w_down, marks,
    normed_out, result_out, token_out, gains_out, att_out, out_out, gu_out, dn_out,
    normed, cots, second, part, got, passed, near, work, att_two, own_out, aq, ao, d_att, wo,
    gu, gu_own, dn, d_gu, d_dn, own, grad_hidden, q, kv, prob, mix, cosine, sine,
    marks_two, gains, middle_all, back_all, total, grad_mix, grad_kv, far_kv,
    gu_in, dn_in, att_in, out_in, gain_c, gain_y, gain_x, gain_z,
    ready, send_sem, recv_sem,
):
    spot = Spot()
    wires = Wires(send_sem, recv_sem)
    x, y, z, c = spot.x, spot.y, spot.z, spot.c
    neighbours = (
        around(spot, "xyz")
        + [spot.along(a, 2) for a in "xyz"]
        + [spot.partner]
        + [spot.in_quad(by)[1] for by in (1, 2, 3)]
    )
    greet(neighbours)

    def tell(which, devices):
        for who in devices:
            pl.semaphore_signal(ready.at[which], inc=1, device_id=who, device_id_type=MESH)

    def hear(which, count):
        pl.semaphore_wait(ready.at[which], count)

    for i, gain in enumerate((gain_attn, gain_mlp)):
        gains[i : i + 1, :] = jnp.concatenate([gain[j : j + 1, :] for j in range(12)], axis=1)

    def normalise(span):
        rows = tokens[span, :].astype(F32)
        own[span, :] = (rows * norm_scale(rows) * gains[0:1, :]).astype(BF16)

    over_rows(0, OWN, normalise)

    def three(first):
        return lambda r, k: r + first == k

    columns = (
        dot(w_query[...], picks(192, 384, three(0)), 1, 0)
        + dot(w_key[...], picks(96, 384, three(192)), 1, 0)
        + dot(w_value[...], picks(96, 384, three(288)), 1, 0)
    )
    att_two[0] = columns.astype(BF16)
    own_out[0] = jnp.zeros((16, D), BF16)
    own_out[0, 0:12] = w_out[...]
    greeted(neighbours)

    swaps = [
        wires.send(att_two.at[0], att_two.at[1], spot.partner),
        wires.send(own_out.at[0], own_out.at[1], spot.partner),
    ]
    rows_y = [PairGather(wires, spot, "y", normed, own, s, n) for s, n in TWO]
    for g in rows_y:
        g.start()
    marks_kept = wires.move(marks, marks_two.at[c])
    marks_got = wires.send(marks, marks_two.at[c], spot.sibling)

    order = picks(512, 512, lambda r, k: quad_order(r) == k)
    for shard, first in ((w_gate, 0), (w_up, 128)):
        moved = dot(shard[...], order, 1, 0).astype(BF16)
        for i in range(4):
            gu_own[i, :, first : first + 128] = moved[:, i * 128 : i * 128 + 128]
    gu_lanes = whole(y, 256)
    gu_here = gu.at[whole(z * 4 + spot.quad, 96), gu_lanes]
    gu_kept = wires.move(gu_own.at[spot.quad], gu_here)
    gu_swap = []
    for by in (1, 2, 3):
        other, who = spot.in_quad(by)
        gu_swap.append(wires.send(gu_own.at[other], gu_here, who))

    def trig(core):
        def step(i):
            span = whole(i, 128)
            row, lane = grid_of(128, 128)
            number = marks_two[core, pl.ds(spot.high * 6 + i, 1), :]
            ones = jnp.ones((128, 128), BF16)
            where = jnp.zeros((128, 128), F32)
            for digit, factor in ((number >> 5, 32.0), (number & 31, 1.0)):
                spread = jnp.where(row == lane, digit.astype(F32), 0.0).astype(BF16)
                where = where + factor * dot(spread, ones, 1, 0)
            grad_kv[core, span, 0:128] = where
            turns = jnp.where(lane < 48, lane, lane - 48).astype(F32) * (2.0 / HD)
            angle = where * jnp.exp(-math.log(ROPE_BASE) * turns)
            inside = lane < HD
            cosine[core, span, :] = jnp.where(inside, jnp.cos(angle), 0.0)
            wave = jnp.sin(angle)
            sine[core, span, :] = jnp.where(inside, jnp.where(lane < 48, -wave, wave), 0.0)

        repeat(6, step)

    marks_kept.wait()
    trig(c)
    for copy in swaps:
        copy.wait_recv()

    def slot_of(pos):
        return (pos % 2) * 2 + pos // 2

    slot = slot_of(x)
    pick = jnp.where(spot.high == c, 0, 1)
    low, high = pl.ds(0, 48), pl.ds(48, 48)
    att_kept = [
        wires.move(att_two.at[pick], aq.at[z, slot]),
        wires.move(own_out.at[pick], ao.at[z, slot]),
    ]
    att_side, out_side = [], []
    for by in (1, -1, 2):
        att_side.append(
            wires.send(att_two.at[pick, low], aq.at[z, slot, low], spot.along("z", by))
        )
        att_side.append(
            wires.send(att_two.at[pick, high], aq.at[z, slot, high], spot.along("x", by))
        )
    for by in (1, -1, 2):
        out_side.append(wires.send(own_out.at[pick], ao.at[z, slot], spot.along("x", by)))
    att_line = [
        RingGather(wires, spot, "x", lambda pos, h: aq.at[pl.ds(2 * h, 2), slot_of(pos), low]),
        RingGather(wires, spot, "z", lambda pos, h: aq.at[pos, pl.ds(2 * h, 2), high]),
    ]
    out_line = RingGather(wires, spot, "z", lambda pos, h: ao.at[pos, pl.ds(2 * h, 2)])
    cot_x = [PairGather(wires, spot, "x", cots, cot, s, n) for s, n in TWO]
    marks_got.wait_recv()
    trig(1 - c)
    for copy in att_kept:
        copy.wait()
    for copy in att_side:
        copy.wait_recv()
    for line in att_line:
        line.start()
    for g in rows_y:
        g.forward()
    rows_y[0].near()
    for line in att_line:
        line.forward()
    for copy in out_side:
        copy.wait_recv()
    out_line.start()
    dn_here = dn.at[y, z]
    dn_kept = wires.move(w_down, dn_here)
    dn_side = [wires.send(w_down, dn_here, spot.along("z", by)) for by in (1, -1, 2)]
    cot_x[0].start()
    rows_y[1].near()
    for line in att_line:
        line.near()
        line.far()

    def out_row(r, k):
        unit = jnp.where(r < 128, r, r - 32)
        real = (r < 96) | ((r >= 128) & (r < 224))
        return real & (unit + ((unit * 5462) >> 16) * 4 == k)

    def project(core, pos):
        both = dot(normed[core, pos], aq[...].reshape(D, 384), 1, 0)
        span = whole(pos, OWN)
        cos, sin = cosine[core, span, :], sine[core, span, :]
        tile = [both[:, 128 * i : 128 * i + 128] for i in range(3)]
        lane = lax.broadcasted_iota(jnp.int32, tile[0].shape, 1)

        def turned(values):
            return (values * cos + swap_halves(values) * sin).astype(BF16)

        q[core, span, 0:128] = turned(tile[0])
        q[core, span, 128:256] = turned(
            jnp.where(lane < 32, pltpu.roll(tile[0], 32, 1), pltpu.roll(tile[1], 32, 1))
        )
        after = pl.ds(pl.multiple_of(WIN + pos * OWN, 64), OWN)
        kv[core, after, 0:128] = turned(
            jnp.where(lane < 64, pltpu.roll(tile[1], 64, 1), pltpu.roll(tile[2], 64, 1))
        )
        kv[core, after, 128:256] = jnp.where(lane < HD, pltpu.roll(tile[2], 96, 1), 0.0).astype(
            BF16
        )

    for g in rows_y:
        g.kept.wait()
    repeat(3, lambda i: project(c, turn(y, i - 1)))
    for g in rows_y:
        for copy in g.shared[:3]:
            copy.wait_recv()
    repeat(3, lambda i: project(1 - c, turn(y, i - 1)))
    for g in rows_y:
        g.far()
    gu_kept.wait()
    for copy in gu_swap:
        copy.wait_recv()
    gu_side = RingGather(
        wires, spot, "y", lambda pos, h: gu.at[whole(z * 2 + h, 192), whole(pos, 256)]
    )
    gu_side.start()
    out_line.forward()
    project(c, turn(y, 2))
    for g in rows_y:
        g.shared[3].wait_recv()
    project(1 - c, turn(y, 2))
    kv_got = wires.send(kv.at[:, pl.ds(768, WIN)], kv.at[:, pl.ds(0, WIN)], spot.along("x", 2))
    normed_kept = wires.move(normed, normed_out)
    left = wires.started()
    cot_x[0].forward()
    cot_x[0].near()
    dn_kept.wait()
    for copy in dn_side:
        copy.wait_recv()
    dn_line = RingGather(wires, spot, "y", lambda pos, h: dn.at[pos, pl.ds(2 * h, 2)])
    gu_line = RingGather(
        wires, spot, "z", lambda pos, h: gu.at[whole(pos, 384), pl.ds(h * 512, 512)]
    )

    scale = HD ** (-0.5)

    def attend(core, run, head):
        span = whole(run, WIN)
        lanes = whole(head, 128)
        window = pl.ds(pl.multiple_of(run * WIN, WIN), SEQ)
        scores = dot(q[core, span, lanes], kv[core, window, 0:128], 1, 1) * scale
        row, column = grid_of(WIN, SEQ)
        spot_of = spot.high * HALF + run * WIN + row[:, 0:1]
        begin = jnp.maximum(
            (spot_of >> 9) << 9, spot_of - grad_kv[core, span, 0:1].astype(jnp.int32)
        )
        begin = begin - (spot.high * HALF + run * WIN) + WIN
        allowed = (column >= begin) & (column <= row + WIN)
        scores = jnp.where(allowed, scores, MASKED)
        weights = jnp.exp(scores - jnp.max(scores, axis=-1, keepdims=True))
        share = weights / jnp.sum(weights, axis=-1, keepdims=True)
        rounded = share.astype(BF16)
        prob[core, run, head] = rounded
        values = dot(rounded, kv[core, window, 128:256], 1, 0)
        mix[core, span, lanes] = values.astype(BF16)

    repeat(4, lambda i: attend(i // 2, 1, i % 2))
    gu_side.forward()
    dn_line.start()
    repeat(4, lambda i: attend(i // 2, 2, i % 2))
    gu_side.near()
    gu_side.far()
    gu_line.start()
    out_line.near()
    out_line.far()
    out_rows = picks(256, 256, out_row)
    wo[...] = dot(out_rows, ao[...].reshape(256, D), 1, 0).astype(BF16).reshape(4, 4, 16, D)

    def project_out(core, half):
        rows = mix[core, half * 384 : half * 384 + 384, :]
        out = dot(rows, wo[...].reshape(256, D), 1, 0).astype(BF16)
        part[core, half * 2 : half * 2 + 2] = out.reshape(2, OWN, D)

    def share_all(sums):
        for s in sums:
            s.share()

    def back_hidden(s):
        def step(core):
            rows = cots[core, :, pl.ds(s * 64, 64)].reshape(256, D)
            grad_hidden[core * 3 + s] = dot(rows, dn[...].reshape(512, D), 1, 1).astype(BF16)

        repeat(2, step)

    sums_y = [PairScatter(wires, spot, "y", part, got, passed, near, s, n) for s, n in THREE]
    rows_x = [PairGather(wires, spot, "x", second, own, s, n) for s, n in THREE]
    repeat(2, lambda i: project_out(i, 1))
    kv_got.wait_recv()
    cot_x[1].start()
    repeat(4, lambda i: attend(i // 2, 0, i % 2))
    cot_x[0].far()
    cot_x[0].finish()
    project_out(1 - c, 0)
    share_all(sums_y)
    project_out(c, 0)
    for g in rows_y:
        g.close()
    normed_kept.wait()
    sums_y[0].first()
    sums_y[1].first()
    sums_y[0].direct()
    dn_line.forward()
    cot_x[1].forward()
    sums_y[0].through()
    sums_y[2].first()
    sums_y[1].direct()
    gu_line.forward()
    sums_y[1].through()
    wires.done(left)
    cot_x[1].near()
    sums_y[2].direct()
    dn_line.near()
    dn_line.far()
    cot_x[1].far()
    cot_x[1].finish()

    def middle_rows(s):
        def use(span):
            middle = tokens[span, :].astype(F32) + s.total(span)
            middle_all[span, :] = middle
            own[span, :] = (middle * norm_scale(middle) * gains[1:2, :]).astype(BF16)

        return use

    def gather_next(i):
        s = sums_y[i]
        s.arrive()
        over_rows(s.start_row, s.size, middle_rows(s))
        s.close()
        rows_x[i].start()

    gather_next(0)
    back_hidden(0)
    sums_y[2].through()
    gather_next(1)
    back_hidden(1)
    rows_x[0].forward()
    back_hidden(2)
    rows_x[0].near()
    gather_next(2)
    rows_x[1].forward()
    rows_x[0].far()
    gu_line.near()
    gu_line.far()
    rows_x[0].finish()
    early = wires.started()

    def feed(core, i):
        span = pl.ds(*THREE[i])
        size = 4 * THREE[i][1]
        rows = second[core, :, span].reshape(size, D)
        both = dot(rows, gu[...], 1, 0)
        upstream = grad_hidden[core * 3 + i].astype(F32)
        for j in range(4):
            gate = both[:, j * 256 : j * 256 + 128]
            upward = both[:, j * 256 + 128 : j * 256 + 256]
            sent = upstream[:, j * 128 : j * 128 + 128]
            sigmoid = jax.nn.sigmoid(gate)
            silu = gate * sigmoid
            slope = sigmoid * (1.0 + gate * (1.0 - sigmoid))
            for first, values in (
                (1024 + j * 128, silu * upward),
                (j * 256, sent * upward * slope),
                (j * 256 + 128, sent * silu),
            ):
                rounded = values.astype(BF16).reshape(4, THREE[i][1], 128)
                work[core, :, span, first : first + 128] = rounded
        back = dot(work[core, :, span, 0:1024].reshape(size, 1024), gu[...], 1, 1)
        part[core, :, span] = back.astype(BF16).reshape(4, THREE[i][1], D)

    sums_x = [PairScatter(wires, spot, "x", part, got, passed, near, s, n) for s, n in THREE]
    grads_y = [PairGather(wires, spot, "y", normed, own, s, n) for s, n in THREE]

    def feed_share(i):
        feed(1 - c, i)
        sums_x[i].share()

    wires.again()
    feed_share(0)
    rows_x[1].near()
    feed(c, 0)
    sums_x[0].first()
    rows_x[2].forward()
    rows_x[1].far()
    rows_x[1].finish()
    feed_share(1)
    sums_x[0].direct()
    rows_x[2].near()
    feed(c, 1)
    sums_x[1].first()
    sums_x[0].through()
    rows_x[2].far()
    sums_x[1].direct()
    rows_x[2].finish()
    feed_share(2)
    sums_x[1].through()
    feed(c, 2)
    sums_x[2].first()
    sums_x[2].direct()
    wires.done(early)
    tell(0, [spot.along("z", 1), spot.along("z", -1)])

    def grad_gate_up(i):
        lanes = whole(i, 256)
        rows = second[:, :, :, lanes].reshape(8 * OWN, 256)
        sent = work[:, :, :, 0:1024].reshape(8 * OWN, 1024)
        d_gu[lanes, :] = dot(rows, sent, 0, 0).astype(BF16)

    def grad_down(i):
        lanes = pl.ds(pl.multiple_of(1024 + i * 256, 256), 256)
        rows = work[:, :, :, lanes].reshape(8 * OWN, 256)
        grad = dot(rows, cots[...].reshape(8 * OWN, D), 0, 0).astype(BF16)
        d_dn[pl.ds(i * 2, 2)] = grad.reshape(2, 4, 32, D)

    def down(i):
        rows = work[i // 2, pl.ds((i % 2) * 2, 2), :, 1024:D].reshape(384, 512)
        second[i // 2, pl.ds((i % 2) * 2, 2)] = (
            dot(rows, dn[...].reshape(512, D), 1, 0).astype(BF16).reshape(2, OWN, D)
        )

    def back_rows(s):
        def use(span):
            grad = s.total(span)
            rows = middle_all[span, :]
            inverse = norm_scale(rows)
            back = cot[span, :].astype(F32) + norm_back(grad, rows, inverse, gains[1:2, :])
            back_all[span, :] = back
            own[span, :] = back.astype(BF16)
            fold(total, grad * rows * inverse)

        return use

    def gather_back(i):
        s = sums_x[i]
        s.arrive()
        rows_x[i].close()
        over_rows(s.start_row, s.size, back_rows(s))
        s.close()
        grads_y[i].start()

    def mix_back(i):
        def step(core):
            span = pl.ds(*THREE[i])
            rows = normed[core, :, span].reshape(256, D)
            grad = dot(rows, wo[...].reshape(256, D), 1, 1).astype(BF16)
            for pos in range(4):
                start = pos * OWN + THREE[i][0]
                grad_mix[core, start : start + 64, :] = grad[pos * 64 : pos * 64 + 64]

        repeat(2, step)

    total[...] = jnp.zeros_like(total)
    repeat(2, grad_gate_up)
    gather_back(0)
    repeat(2, lambda i: grad_gate_up(2 + i))
    sums_x[2].through()
    grads_y[0].forward()
    repeat(2, lambda i: grad_gate_up(4 + i))
    hear(0, 2)
    gu_sum = [
        LineScatter(
            wires, spot, "z",
            lambda pos, h, lot=lot: d_gu.at[whole(pos * 4 + lot * 2 + h, 96)],
            lambda h, lot=lot: gu.at[pl.ds(lot * 192 + h * 96, 96)],
            lambda h, lot=lot: gu.at[pl.ds(384 + lot * 192 + h * 96, 96)],
            lambda side, h, lot=lot: gu.at[pl.ds(768 + side * 384 + lot * 192 + h * 96, 96)],
        )
        for lot in (0, 1)
    ]
    gu_got = []

    def gu_beside(lot):
        gu_sum[lot].finish()
        for by in (1, -1, 2):
            part_of = d_gu.at[whole(z * 2 + lot, 192), whole(turn(y, by), 256)]
            into = gu_in.at[y, pl.ds(lot * 192, 192)]
            gu_got.append(wires.send(part_of, into, spot.along("y", by)))

    gu_sum[0].first()
    gather_back(1)
    grads_y[0].near()
    repeat(2, grad_down)
    grads_y[1].forward()
    grads_y[0].far()
    gather_back(2)
    repeat(2, down)
    gu_sum[0].second()
    gu_sum[1].first()
    grads_y[1].near()
    grads_y[2].forward()
    repeat(2, lambda i: down(2 + i))
    tell(1, around(spot, "xy") + [spot.along("z", 1), spot.along("z", -1)])
    again = wires.move(normed_out, cots)
    gain_c[c, 1:2] = jnp.sum(total[...], axis=0, keepdims=True)
    grads_y[0].finish()
    mix_back(0)
    grads_y[1].far()
    grads_y[2].near()
    grads_y[1].finish()
    mix_back(1)
    hear(1, 7)
    sums_m = [
        PairScatter(
            wires, spot, "x", second, work.at[0], work.at[1, 0], work.at[1, pl.ds(1, 2)], s, n
        )
        for s, n in TWO
    ]
    share_all(sums_m)
    grad_kv[...] = jnp.zeros_like(grad_kv)
    grads_y[2].far()
    grads_y[2].finish()
    mix_back(2)
    left = wires.started()
    gu_beside(0)

    def attend_back(core, run, head):
        span = whole(run, WIN)
        lanes = whole(head, 128)
        window = pl.ds(pl.multiple_of(run * WIN, WIN), SEQ)
        rounded = prob[core, run, head]
        share = rounded.astype(F32)
        mixed = grad_mix[core, span, lanes]
        asked = q[core, span, lanes]
        grad = dot(mixed, kv[core, window, 128:256], 1, 1)
        inner = jnp.sum(share * grad, axis=-1, keepdims=True)
        scored = (share * (grad - inner)).astype(BF16)
        grad_kv[core, window, 0:128] += dot(scored, asked, 0, 0) * scale
        grad_kv[core, window, 128:256] += dot(rounded, mixed, 0, 0)
        grad_q = dot(scored, kv[core, window, 0:128], 1, 0) * scale
        cos, sin = cosine[core, span, :], sine[core, span, :]
        q[core, span, lanes] = (grad_q * cos - swap_halves(grad_q) * sin).astype(BF16)

    repeat(4, lambda i: attend_back(i // 2, 0, i % 2))
    far_from = grad_mix.at[:, pl.ds(0, WIN)]
    for core in (0, 1):
        far_from[core] = grad_kv[core, 0:WIN, :].astype(BF16)
    far_got = wires.send(far_from, far_kv, spot.along("x", 2))
    for s in sums_m:
        s.first()
    gu_sum[1].second()
    dn_sum = LineScatter(
        wires, spot, "z",
        lambda pos, h: d_dn.at[pl.ds(2 * h, 2), pos],
        lambda h: dn.at[0, pl.ds(2 * h, 2)],
        lambda h: dn.at[1, pl.ds(2 * h, 2)],
        lambda side, h: dn.at[2 + side, pl.ds(2 * h, 2)],
    )
    dn_sum.first()
    repeat(4, lambda i: attend_back(i // 2, 1, i % 2))
    for s in sums_m:
        s.direct()
    repeat(4, lambda i: attend_back(i // 2, 2, i % 2))
    gu_beside(1)

    def out_rows_back(r, k):
        unit = jnp.where(k < 128, k, k - 32)
        real = (k < 96) | ((k >= 128) & (k < 224))
        return real & (unit + ((unit * 5462) >> 16) * 4 == r)

    grad_out = dot(mix[...].reshape(8 * OWN, 256), normed[...].reshape(8 * OWN, D), 0, 0)
    grad_out = dot(picks(256, 256, out_rows_back), grad_out.astype(BF16), 1, 0)
    wo[...] = grad_out.astype(BF16).reshape(4, 4, 16, D)
    out_sum = LineScatter(
        wires, spot, "z",
        lambda pos, h: wo.at[pos, pl.ds(2 * h, 2)],
        lambda h: ao.at[0, pl.ds(2 * h, 2)],
        lambda h: ao.at[1, pl.ds(2 * h, 2)],
        lambda side, h: ao.at[2 + side, pl.ds(2 * h, 2)],
    )
    out_sum.first()
    far_got.wait_recv()
    for core in (0, 1):
        grad_kv[core, 768:1024, :] += far_kv[core].astype(F32)

    def turn_back(i):
        core, pos = i // 4, i % 4
        after = pl.ds(pl.multiple_of(WIN + pos * OWN, 64), OWN)
        span = whole(pos, OWN)
        cos, sin = cosine[core, span, :], sine[core, span, :]
        keyed = grad_kv[core, after, 0:128]
        keyed = pltpu.roll(keyed * cos - swap_halves(keyed) * sin, 64, 1)
        valued = pltpu.roll(grad_kv[core, after, 128:256], 32, 1)
        front = q[core, span, 0:128].astype(F32)
        behind = pltpu.roll(q[core, span, 128:256].astype(F32), 96, 1)
        lane = lax.broadcasted_iota(jnp.int32, front.shape, 1)
        q[core, span, 0:128] = jnp.where(lane < 96, front, behind).astype(BF16)
        q[core, span, 128:256] = jnp.where(lane < 64, behind, keyed).astype(BF16)
        kv[core, after, 0:128] = jnp.where(lane < 32, keyed, valued).astype(BF16)

    repeat(8, turn_back)

    def normed_back(core):
        def step(pos):
            after = pl.ds(pl.multiple_of(WIN + pos * 384, 128), 384)
            rows = jnp.concatenate([q[core, whole(pos, 384), :], kv[core, after, 0:128]], axis=1)
            grad = dot(rows, aq[...].reshape(D, 384), 1, 1).astype(BF16)
            part[core, pl.ds(pos * 2, 2)] = grad.reshape(2, OWN, D)

        repeat(2, step)

    sums_n = [PairScatter(wires, spot, "y", part, got, passed, near, s, n) for s, n in THREE]
    normed_back(1 - c)
    share_all(sums_n)
    normed_back(c)
    sums_n[0].first()
    sums_n[1].first()
    sums_n[0].direct()
    dn_sum.second()
    again.wait()

    def grad_columns(i):
        rows = cots[:, :, :, whole(i, 384)].reshape(8 * OWN, 384)
        asked = dot(rows, q[...].reshape(8 * OWN, 256), 0, 0)
        other = dot(rows, kv[:, pl.ds(WIN, HALF), 0:128].reshape(8 * OWN, 128), 0, 0)
        d_att[i, :, :, 0:256] = asked.astype(BF16).reshape(4, 96, 256)
        d_att[i, :, :, 256:384] = other.astype(BF16).reshape(4, 96, 128)
        held = aq[i].reshape(384, 384).astype(F32)
        folded = (
            held[:, 0:128] * asked[:, 0:128]
            + held[:, 128:256] * asked[:, 128:256]
            + held[:, 256:384] * other
        )
        gain_c[c, 0:1, whole(i, 384)] = jnp.sum(folded.T, axis=0, keepdims=True)

    repeat(2, grad_columns)
    sums_n[0].through()
    sums_n[2].first()
    sums_n[1].direct()
    for s in sums_m:
        s.through()
    repeat(2, lambda i: grad_columns(2 + i))
    gain_c[c, 0:1] = gain_c[c, 0:1] / gains[0:1, :]
    tell(2, [spot.along(a, by) for a in "xz" for by in (1, -1)])
    gain_got = [wires.send(gain_c.at[c], gain_c.at[c], spot.sibling)]
    sums_n[1].through()
    sums_n[2].direct()
    wires.done(left)
    hear(2, 4)
    att_sum = [
        LineScatter(
            wires, spot, "x",
            lambda pos, h: d_att.at[pl.ds(2 * h, 2), slot_of(pos), low],
            lambda h: aq.at[0, pl.ds(2 * h, 2), low],
            lambda h: aq.at[1, pl.ds(2 * h, 2), low],
            lambda side, h: aq.at[2 + side, pl.ds(2 * h, 2), low],
        ),
        LineScatter(
            wires, spot, "z",
            lambda pos, h: d_att.at[pos, pl.ds(2 * h, 2), high],
            lambda h: aq.at[0, pl.ds(2 * h, 2), high],
            lambda h: aq.at[1, pl.ds(2 * h, 2), high],
            lambda side, h: aq.at[2 + side, pl.ds(2 * h, 2), high],
        ),
    ]
    for line in att_sum:
        line.first()
    out_sum.second()

    def add_gains(held, axis, into):
        for copy in gain_got:
            copy.wait_recv()
        summed = held[0]
        for i in range(1, held.shape[0]):
            summed = summed + held[i]
        if into is None:
            gains_out[...] = summed
            return []
        me = spot.me(axis)
        into[me] = summed
        return [wires.send(into.at[me], into.at[me], spot.along(axis, by)) for by in (1, -1, 2)]

    gain_got = add_gains(gain_c, "x", gain_x)
    for line in att_sum:
        line.second()
    sums_n[2].through()
    dn_sum.finish()
    dn_got = [
        wires.send(d_dn.at[turn(y, by), z], dn_in.at[y], spot.along("y", by))
        for by in (1, -1, 2)
    ]
    gain_got = add_gains(gain_x, "z", gain_z)

    for copy in gu_got:
        copy.wait_recv()
    mine = d_gu.at[whole(z, 384), whole(y, 256)]
    add_into(mine, mine, *[gu_in.at[turn(y, by)] for by in (1, -1, 2)])
    gu_done = []
    for by in (1, 2, 3):
        other, who = spot.in_quad(by)
        rows = d_gu.at[whole(z * 4 + other, 96), whole(y, 256)]
        gu_done.append(wires.send(rows, gu_own.at[spot.quad], who))

    def token_rows(s):
        def use(span):
            grad = s.total(span)
            rows = tokens[span, :].astype(F32)
            inverse = norm_scale(rows)
            out = back_all[span, :] + norm_back(grad, rows, inverse, gains[0:1, :])
            part[c, y, span] = out.astype(BF16)

        return use

    def result_rows(s):
        def use(span):
            second[c, x, span] = (middle_all[span, :] + s.total(span)).astype(BF16)

        return use

    token_kept = []

    def token_part(i):
        s = sums_n[i]
        s.arrive()
        over_rows(s.start_row, s.size, token_rows(s))
        token_kept.append(wires.move(part.at[c, y, s.rows()], token_out.at[s.rows()]))

    def result_part(s):
        s.arrive()
        over_rows(s.start_row, s.size, result_rows(s))

    for s in sums_m:
        result_part(s)
    result_kept = wires.move(second.at[c, x], result_out)
    att_got = []
    for line in att_sum:
        line.finish()
    out_sum.finish()
    for by in (1, -1, 2):
        far, who = turn(z, by), spot.along("z", by)
        att_got.append(wires.send(d_att.at[far, slot, low], att_in.at[z, low], who))
        far, who = slot_of(turn(x, by)), spot.along("x", by)
        att_got.append(wires.send(d_att.at[z, far, high], att_in.at[x, high], who))
        att_got.append(wires.send(wo.at[z, far], out_in.at[x], who))
    token_part(0)
    gain_got = add_gains(gain_z, "y", gain_y)
    kept_rows = d_gu.at[whole(z * 4 + spot.quad, 96), whole(y, 256)]
    gu_out[spot.quad] = kept_rows[...]
    for copy in att_got:
        copy.wait_recv()
    for span, me in ((low, z), (high, x)):
        others = [att_in.at[turn(me, by), span] for by in (1, -1, 2)]
        add_into(att_two.at[0, span], d_att.at[z, slot, span], *others)
    others = [out_in.at[turn(x, by)] for by in (1, -1, 2)]
    add_into(own_out.at[0], wo.at[z, slot], *others)
    swaps = [
        wires.send(att_two.at[0], att_two.at[1], spot.partner),
        wires.send(own_out.at[0], own_out.at[1], spot.partner),
    ]
    token_part(1)
    for copy in gu_done:
        copy.wait_recv()
    for by in (1, 2, 3):
        other = turn(spot.quad, by)
        gu_out[other] = gu_own[other]
    for copy in dn_got:
        copy.wait_recv()
    add_into(
        dn_out, d_dn.at[y, z], *[dn_in.at[turn(y, by)] for by in (1, -1, 2)]
    )
    token_part(2)
    add_gains(gain_y, None, None)
    for copy in swaps:
        copy.wait_recv()
    att_out[...] = att_two[pick]
    out_out[...] = own_out[pick]
    result_kept.wait()
    for copy in token_kept:
        copy.wait()
    wires.close()


def finish_kernel(
    result, token, gains, att, out, gu, dn,
    result_out, token_out, attn_out, mlp_out, query_out, key_out, value_out, out_out,
    gate_out, up_out, dn_out,
):
    result_out[...] = result[...]
    token_out[...] = token[...]
    for i, into in enumerate((attn_out, mlp_out)):
        for j in range(12):
            into[j : j + 1, :] = gains[i : i + 1, j * 128 : j * 128 + 128]
    rows = att[...]

    def three(first):
        return lambda r, k: r == k + first

    query_out[...] = dot(rows, picks(384, 192, three(0)), 1, 0)
    key_out[...] = dot(rows, picks(384, 96, three(192)), 1, 0)
    value_out[...] = dot(rows, picks(384, 96, three(288)), 1, 0)
    out_out[...] = out[0:12, :].astype(F32)
    order = picks(512, 512, lambda r, k: quad_order(k) == r)
    for first, into in ((0, gate_out), (128, up_out)):
        moved = jnp.concatenate([gu[i, :, first : first + 128] for i in range(4)], axis=1)
        into[...] = dot(moved, order, 1, 0)
    dn_out[...] = dn[...]


def layer_call(
    tokens, gain_attn, gain_mlp, cot, w_query, w_key, w_value, w_out, w_gate, w_up, w_down, marks
):
    sends, receives = 120, 170
    shape = jax.ShapeDtypeStruct
    outs = (
        (shape((2, 4, OWN, D), BF16), ANY),
        (shape((OWN, D), BF16), ANY),
        (shape((OWN, D), BF16), ANY),
        (shape((2, D), F32), VMEM),
        (shape((96, 384), BF16), VMEM),
        (shape((16, D), BF16), VMEM),
        (shape((4, 96, 256), BF16), VMEM),
        (shape((32, D), F32), VMEM),
    )
    scratch = [
        ((2, 4, OWN, D), BF16),
        ((2, 4, OWN, D), BF16),
        ((2, 4, OWN, D), BF16),
        ((2, 4, OWN, D), BF16),
        ((4, OWN, D), BF16),
        ((OWN, D), BF16),
        ((2, OWN, D), BF16),
        ((2, 4, OWN, D), BF16),
        ((2, 96, 384), BF16),
        ((2, 16, D), BF16),
        ((4, 4, 96, 384), BF16),
        ((4, 4, 16, D), BF16),
        ((4, 4, 96, 384), BF16),
        ((4, 4, 16, D), BF16),
        ((D, 1024), BF16),
        ((4, 96, 256), BF16),
        ((4, 4, 32, D), BF16),
        ((D, 1024), BF16),
        ((4, 4, 32, D), BF16),
        ((OWN, D), BF16),
        ((6, 256, 512), BF16),
        ((2, HALF, 256), BF16),
        ((2, HALF + WIN, 256), BF16),
        ((2, 3, 2, WIN, SEQ), BF16),
        ((2, HALF, 256), BF16),
        ((2, HALF, 128), F32),
        ((2, HALF, 128), F32),
        ((2, 12, 128), jnp.int32),
        ((2, D), F32),
        ((OWN, D), F32),
        ((OWN, D), F32),
        ((8, D), F32),
        ((2, HALF, 256), BF16),
        ((2, HALF + WIN, 256), F32),
        ((2, WIN, 256), BF16),
        ((4, 384, 256), BF16),
        ((4, 32, D), BF16),
        ((4, 96, 384), BF16),
        ((4, 16, D), BF16),
        ((2, 2, D), F32),
        ((4, 2, D), F32),
        ((4, 2, D), F32),
        ((4, 2, D), F32),
    ]
    outs_raw = pl.pallas_call(
        layer_kernel,
        out_shape=tuple(o[0] for o in outs),
        in_specs=[VMEM] * 12,
        out_specs=[o[1] for o in outs],
        scratch_shapes=[pltpu.VMEM(*s) for s in scratch]
        + [
            pltpu.SemaphoreType.REGULAR((3,)),
            pltpu.SemaphoreType.DMA((sends,)),
            pltpu.SemaphoreType.DMA((receives,)),
        ],
        compiler_params=pltpu.CompilerParams(
            collective_id=1, has_side_effects=True, vmem_limit_bytes=64 << 20
        ),
        name="layer",
    )(tokens, gain_attn, gain_mlp, cot, w_query, w_key, w_value, w_out, w_gate, w_up, w_down, marks)
    finals = (
        shape((OWN, D), BF16),
        shape((OWN, D), BF16),
        shape((12, 128), F32),
        shape((12, 128), F32),
        shape((96, 192), F32),
        shape((96, 96), F32),
        shape((96, 96), F32),
        shape((12, D), F32),
        shape((96, 512), F32),
        shape((96, 512), F32),
        shape((32, D), F32),
    )
    return pl.pallas_call(
        finish_kernel,
        out_shape=finals,
        in_specs=[VMEM] * 7,
        out_specs=[VMEM] * 11,
        name="finish",
    )(*outs_raw[1:])


def shards(
    tokens,
    gain_attn,
    gain_mlp,
    w_query,
    w_key,
    w_value,
    w_out,
    w_gate,
    w_up,
    w_down,
    segments,
    positions,
    cotangent,
):
    del segments
    done = layer_call(
        tokens,
        gain_attn.reshape(12, 128),
        gain_mlp.reshape(12, 128),
        cotangent,
        w_query,
        w_key,
        w_value,
        w_out,
        w_gate,
        w_up,
        w_down,
        positions.reshape(12, 128),
    )
    return (*done[:2], done[2].reshape(D), done[3].reshape(D), *done[4:])


def solution(mesh):
    placed = (
        P(("dp", "tensor"), None),
        P(),
        P(),
        P("dp", "tensor"),
        P("dp", "tensor"),
        P("dp", "tensor"),
        P(("tensor", "dp"), None),
        P("dp", "tensor"),
        P("dp", "tensor"),
        P(("tensor", "dp"), None),
        P("dp"),
        P("dp"),
        P(("dp", "tensor"), None),
    )
    return jax.shard_map(
        shards,
        mesh=mesh,
        in_specs=placed,
        out_specs=(
            P(("dp", "tensor"), None),
            P(("dp", "tensor"), None),
            P(),
            P(),
            P("dp", "tensor"),
            P("dp", "tensor"),
            P("dp", "tensor"),
            P(("tensor", "dp"), None),
            P("dp", "tensor"),
            P("dp", "tensor"),
            P(("tensor", "dp"), None),
        ),
        check_vma=False,
    )
```

time: 227 us -> 191 us (0.84)
  Pallas kernels: 226 us -> 190 us
    pallas_call x1, Pallas kernels: 223 us -> 187 us  [layer_call(): pl.pallas_call(layer_kernel, out_shape=tuple((o[0] for o in outs)), in_sp...]
where the time goes in v1:
time: 191 us
  Pallas kernels  190 us (99%)
    pallas_call x1, Pallas kernels, layer_call(): pl.pallas_call(layer_kernel, out_shape=tuple((o[0] for o in outs)), in_sp...  187 us

profile of v1, /device:TPU:1, one launch (start us, length us, event | category | flops | bytes accessed | tf_op | source)
XLA Modules:
  0.0 190.8 jit_solution(2282943388180198280)
XLA Ops:
  0.6 187.0 %layer.1 = (bf16[2,4,192,1536]{3,2,1,0:T(8,128)(2,1)}, bf16[192,1536]{1,0:T(8,128)(2,1)}, bf16[192,1536]{1,0:T(8,128)(2,1)}, f32[2,1536]{1,0:T(2,128)}, bf16[96,...) custom-call(bf16[192,1536]{1,0:T(8,128)(2,1)} %tokens.1, ...), custom_call_target="tpu_custom_call" | custom-call | tf_op jit(solution)/shard_map/layer/pallas_call | solution.py:1249
  187.6 3.1 %finish.1 = (bf16[192,1536]{1,0:T(8,128)(2,1)}, bf16[192,1536]{1,0:T(8,128)(2,1)}, f32[12,128]{1,0:T(8,128)}, f32[12,128]{1,0:T(8,128)}, f32[96,192]{1,0:T(8,128...) custom-call(bf16[192,1536]{1,0:T(8,128)(2,1)} %get-tuple-element.29., ...), custom_call_target="tpu_custom_call" | custom-call | tf_op jit(solution)/shard_map/finish/pallas_call | solution.py:1278

commit v2 on v1

--- a/solution.py
+++ b/solution.py
@@ -160,12 +160,19 @@
         self.next, self.prev = spot.along(axis, 1), spot.along(axis, -1)
 
     def start(self, own=None):
-        own = own or (lambda half: self.at(self.me, half))
+        self.own = own or (lambda half: self.at(self.me, half))
         send, at, me = self.wires.send, self.at, self.me
-        self.right0 = send(own(0), at(me, 0), self.next)
-        self.left1 = send(own(1), at(me, 1), self.prev)
-        self.right1 = send(own(1), at(me, 1), self.next)
-        self.left0 = send(own(0), at(me, 0), self.prev)
+        self.right0 = send(self.own(0), at(me, 0), self.next)
+        self.left1 = send(self.own(1), at(me, 1), self.prev)
+
+    def rest(self):
+        send, at, me = self.wires.send, self.at, self.me
+        self.right1 = send(self.own(1), at(me, 1), self.next)
+        self.left0 = send(self.own(0), at(me, 0), self.prev)
+
+    def begin(self):
+        self.start()
+        self.rest()
 
     def forward(self):
         send, at, me = self.wires.send, self.at, self.me
@@ -215,6 +222,9 @@
         self.shared = [self.wires.send(mine, place_of, self.spot.sibling)]
         self.kept = self.wires.move(mine, place_of)
 
+    def rest(self):
+        self.ring.rest()
+
     def forward(self):
         self.ring.forward()
 
@@ -268,6 +278,12 @@
         self.pass1 = self.wires.send(
             self.got.at[pos, self.rows(1)], self.passed.at[self.rows(1)], self.prev
         )
+
+    def left(self):
+        self.wires.done([self.pass0, self.pass1])
+
+    def gone(self):
+        self.wires.done(self.arriving)
 
     def direct(self):
         self.arriving = []
@@ -416,7 +432,7 @@
 
 def layer_kernel(
     tokens, gain_attn, gain_mlp, cot, w_query, w_key, w_value, w_out, w_gate, w_up, w_down, marks,
-    normed_out, result_out, token_out, gains_out, att_out, out_out, gu_out, dn_out,
+    normed_out, result_out, token_out, gains_out, att_out, out_out, gate_out, up_out, dn_out,
     normed, cots, second, part, got, passed, near, work, att_two, own_out, aq, ao, d_att, wo,
     gu, gu_own, dn, d_gu, d_dn, own, grad_hidden, q, kv, prob, mix, cosine, sine,
     marks_two, gains, middle_all, back_all, total, grad_mix, grad_kv, far_kv,
@@ -531,6 +547,8 @@
         )
     for by in (1, -1, 2):
         out_side.append(wires.send(own_out.at[pick], ao.at[z, slot], spot.along("x", by)))
+    for g in rows_y:
+        g.rest()
     att_line = [
         RingGather(wires, spot, "x", lambda pos, h: aq.at[pl.ds(2 * h, 2), slot_of(pos), low]),
         RingGather(wires, spot, "z", lambda pos, h: aq.at[pos, pl.ds(2 * h, 2), high]),
@@ -544,7 +562,7 @@
     for copy in att_side:
         copy.wait_recv()
     for line in att_line:
-        line.start()
+        line.begin()
     for g in rows_y:
         g.forward()
     rows_y[0].near()
@@ -552,11 +570,18 @@
         line.forward()
     for copy in out_side:
         copy.wait_recv()
-    out_line.start()
+    out_line.begin()
     dn_here = dn.at[y, z]
     dn_kept = wires.move(w_down, dn_here)
-    dn_side = [wires.send(w_down, dn_here, spot.along("z", by)) for by in (1, -1, 2)]
+    first_rows, last_rows = pl.ds(0, 16), pl.ds(16, 16)
+    dn_side = []
+    for by in (1, -1, 2):
+        for axis, rows in (("z", first_rows), ("y", last_rows)):
+            dn_side.append(
+                wires.send(w_down.at[rows], dn.at[y, z, rows], spot.along(axis, by))
+            )
     cot_x[0].start()
+    cot_x[0].rest()
     rows_y[1].near()
     for line in att_line:
         line.near()
@@ -604,7 +629,7 @@
     gu_side = RingGather(
         wires, spot, "y", lambda pos, h: gu.at[whole(z * 2 + h, 192), whole(pos, 256)]
     )
-    gu_side.start()
+    gu_side.begin()
     out_line.forward()
     project(c, turn(y, 2))
     for g in rows_y:
@@ -615,10 +640,6 @@
     left = wires.started()
     cot_x[0].forward()
     cot_x[0].near()
-    dn_kept.wait()
-    for copy in dn_side:
-        copy.wait_recv()
-    dn_line = RingGather(wires, spot, "y", lambda pos, h: dn.at[pos, pl.ds(2 * h, 2)])
     gu_line = RingGather(
         wires, spot, "z", lambda pos, h: gu.at[whole(pos, 384), pl.ds(h * 512, 512)]
     )
@@ -647,11 +668,16 @@
 
     repeat(4, lambda i: attend(i // 2, 1, i % 2))
     gu_side.forward()
-    dn_line.start()
+    dn_kept.wait()
+    for copy in dn_side:
+        copy.wait_recv()
+    dn_line = [
+        RingGather(wires, spot, "y", lambda pos, h: dn.at[pos, pl.ds(2 * h, 2), first_rows]),
+        RingGather(wires, spot, "z", lambda pos, h: dn.at[pl.ds(2 * h, 2), pos, last_rows]),
+    ]
+    for line in dn_line:
+        line.begin()
     repeat(4, lambda i: attend(i // 2, 2, i % 2))
-    gu_side.near()
-    gu_side.far()
-    gu_line.start()
     out_line.near()
     out_line.far()
     out_rows = picks(256, 256, out_row)
@@ -676,33 +702,39 @@
     sums_y = [PairScatter(wires, spot, "y", part, got, passed, near, s, n) for s, n in THREE]
     rows_x = [PairGather(wires, spot, "x", second, own, s, n) for s, n in THREE]
     repeat(2, lambda i: project_out(i, 1))
+    gu_side.near()
+    gu_side.far()
+    gu_line.start()
     kv_got.wait_recv()
     cot_x[1].start()
     repeat(4, lambda i: attend(i // 2, 0, i % 2))
-    cot_x[0].far()
-    cot_x[0].finish()
+    cot_x[1].rest()
+    for line in dn_line:
+        line.forward()
     project_out(1 - c, 0)
-    share_all(sums_y)
+    sums_y[0].share()
     project_out(c, 0)
     for g in rows_y:
         g.close()
     normed_kept.wait()
     sums_y[0].first()
+    cot_x[1].forward()
+    gu_line.rest()
+    cot_x[0].far()
+    cot_x[0].finish()
+    sums_y[0].left()
+    sums_y[0].direct()
+    sums_y[1].share()
+    cot_x[1].near()
+    sums_y[0].through()
+    gu_line.forward()
+    cot_x[1].far()
+    sums_y[0].gone()
     sums_y[1].first()
-    sums_y[0].direct()
-    dn_line.forward()
-    cot_x[1].forward()
-    sums_y[0].through()
-    sums_y[2].first()
-    sums_y[1].direct()
-    gu_line.forward()
-    sums_y[1].through()
-    wires.done(left)
-    cot_x[1].near()
-    sums_y[2].direct()
-    dn_line.near()
-    dn_line.far()
-    cot_x[1].far()
+    sums_y[2].share()
+    for line in dn_line:
+        line.near()
+        line.far()
     cot_x[1].finish()
 
     def middle_rows(s):
@@ -721,20 +753,27 @@
         rows_x[i].start()
 
     gather_next(0)
+    sums_y[1].direct()
     back_hidden(0)
+    sums_y[1].through()
+    rows_x[0].rest()
+    grad_kv[...] = jnp.zeros_like(grad_kv)
+    wires.done(left)
+    rows_x[0].forward()
+    sums_y[1].gone()
+    sums_y[2].first()
+    back_hidden(1)
+    gather_next(1)
+    sums_y[2].direct()
+    rows_x[0].near()
+    back_hidden(2)
     sums_y[2].through()
-    gather_next(1)
-    back_hidden(1)
-    rows_x[0].forward()
-    back_hidden(2)
-    rows_x[0].near()
-    gather_next(2)
+    rows_x[1].rest()
+    rows_x[0].far()
     rows_x[1].forward()
-    rows_x[0].far()
     gu_line.near()
     gu_line.far()
     rows_x[0].finish()
-    early = wires.started()
 
     def feed(core, i):
         span = pl.ds(*THREE[i])
@@ -766,28 +805,30 @@
         feed(1 - c, i)
         sums_x[i].share()
 
+    gather_next(2)
+    early = wires.started()
     wires.again()
     feed_share(0)
+    rows_x[2].rest()
     rows_x[1].near()
     feed(c, 0)
+    rows_x[2].forward()
     sums_x[0].first()
-    rows_x[2].forward()
     rows_x[1].far()
+    sums_x[0].direct()
     rows_x[1].finish()
+    rows_x[2].near()
     feed_share(1)
-    sums_x[0].direct()
-    rows_x[2].near()
+    rows_x[2].far()
     feed(c, 1)
     sums_x[1].first()
     sums_x[0].through()
-    rows_x[2].far()
+    rows_x[2].finish()
     sums_x[1].direct()
-    rows_x[2].finish()
     feed_share(2)
-    sums_x[1].through()
     feed(c, 2)
     sums_x[2].first()
-    sums_x[2].direct()
+    sums_x[1].through()
     wires.done(early)
     tell(0, [spot.along("z", 1), spot.along("z", -1)])
 
@@ -841,11 +882,15 @@
         repeat(2, step)
 
     total[...] = jnp.zeros_like(total)
+    gather_back(0)
+    sums_x[2].direct()
     repeat(2, grad_gate_up)
-    gather_back(0)
+    grads_y[0].rest()
     repeat(2, lambda i: grad_gate_up(2 + i))
+    gather_back(1)
+    grads_y[0].forward()
     sums_x[2].through()
-    grads_y[0].forward()
+    grads_y[1].rest()
     repeat(2, lambda i: grad_gate_up(4 + i))
     hear(0, 2)
     gu_sum = [
@@ -868,41 +913,32 @@
             gu_got.append(wires.send(part_of, into, spot.along("y", by)))
 
     gu_sum[0].first()
-    gather_back(1)
     grads_y[0].near()
-    repeat(2, grad_down)
     grads_y[1].forward()
+    gather_back(2)
     grads_y[0].far()
-    gather_back(2)
+    grad_down(0)
+    grads_y[2].rest()
+    grads_y[1].near()
     repeat(2, down)
+    grads_y[2].forward()
+    grads_y[0].finish()
+    mix_back(0)
     gu_sum[0].second()
     gu_sum[1].first()
-    grads_y[1].near()
-    grads_y[2].forward()
+    grads_y[1].far()
+    grad_down(1)
+    grads_y[2].near()
+    grads_y[1].finish()
+    mix_back(1)
+    grads_y[2].far()
     repeat(2, lambda i: down(2 + i))
     tell(1, around(spot, "xy") + [spot.along("z", 1), spot.along("z", -1)])
     again = wires.move(normed_out, cots)
     gain_c[c, 1:2] = jnp.sum(total[...], axis=0, keepdims=True)
-    grads_y[0].finish()
-    mix_back(0)
-    grads_y[1].far()
-    grads_y[2].near()
-    grads_y[1].finish()
-    mix_back(1)
-    hear(1, 7)
-    sums_m = [
-        PairScatter(
-            wires, spot, "x", second, work.at[0], work.at[1, 0], work.at[1, pl.ds(1, 2)], s, n
-        )
-        for s, n in TWO
-    ]
-    share_all(sums_m)
-    grad_kv[...] = jnp.zeros_like(grad_kv)
-    grads_y[2].far()
     grads_y[2].finish()
     mix_back(2)
     left = wires.started()
-    gu_beside(0)
 
     def attend_back(core, run, head):
         span = whole(run, WIN)
@@ -926,9 +962,22 @@
     for core in (0, 1):
         far_from[core] = grad_kv[core, 0:WIN, :].astype(BF16)
     far_got = wires.send(far_from, far_kv, spot.along("x", 2))
-    for s in sums_m:
-        s.first()
     gu_sum[1].second()
+    gu_beside(0)
+    hear(1, 7)
+    sums_m = [
+        PairScatter(
+            wires, spot, "x", second, work.at[0], work.at[1, 0], work.at[1, pl.ds(1, 2)], s, n
+        )
+        for s, n in TWO
+    ]
+    share_all(sums_m)
+    repeat(4, lambda i: attend_back(i // 2, 1, i % 2))
+    sums_m[0].first()
+    sums_m[0].direct()
+    repeat(4, lambda i: attend_back(i // 2, 2, i % 2))
+    sums_m[1].first()
+    sums_m[1].direct()
     dn_sum = LineScatter(
         wires, spot, "z",
         lambda pos, h: d_dn.at[pl.ds(2 * h, 2), pos],
@@ -937,28 +986,6 @@
         lambda side, h: dn.at[2 + side, pl.ds(2 * h, 2)],
     )
     dn_sum.first()
-    repeat(4, lambda i: attend_back(i // 2, 1, i % 2))
-    for s in sums_m:
-        s.direct()
-    repeat(4, lambda i: attend_back(i // 2, 2, i % 2))
-    gu_beside(1)
-
-    def out_rows_back(r, k):
-        unit = jnp.where(k < 128, k, k - 32)
-        real = (k < 96) | ((k >= 128) & (k < 224))
-        return real & (unit + ((unit * 5462) >> 16) * 4 == r)
-
-    grad_out = dot(mix[...].reshape(8 * OWN, 256), normed[...].reshape(8 * OWN, D), 0, 0)
-    grad_out = dot(picks(256, 256, out_rows_back), grad_out.astype(BF16), 1, 0)
-    wo[...] = grad_out.astype(BF16).reshape(4, 4, 16, D)
-    out_sum = LineScatter(
-        wires, spot, "z",
-        lambda pos, h: wo.at[pos, pl.ds(2 * h, 2)],
-        lambda h: ao.at[0, pl.ds(2 * h, 2)],
-        lambda h: ao.at[1, pl.ds(2 * h, 2)],
-        lambda side, h: ao.at[2 + side, pl.ds(2 * h, 2)],
-    )
-    out_sum.first()
     far_got.wait_recv()
     for core in (0, 1):
         grad_kv[core, 768:1024, :] += far_kv[core].astype(F32)
@@ -979,6 +1006,7 @@
         kv[core, after, 0:128] = jnp.where(lane < 32, keyed, valued).astype(BF16)
 
     repeat(8, turn_back)
+    gu_beside(1)
 
     def normed_back(core):
         def step(pos):
@@ -994,8 +1022,6 @@
     share_all(sums_n)
     normed_back(c)
     sums_n[0].first()
-    sums_n[1].first()
-    sums_n[0].direct()
     dn_sum.second()
     again.wait()
 
@@ -1014,18 +1040,17 @@
         gain_c[c, 0:1, whole(i, 384)] = jnp.sum(folded.T, axis=0, keepdims=True)
 
     repeat(2, grad_columns)
-    sums_n[0].through()
+    sums_n[1].first()
     sums_n[2].first()
-    sums_n[1].direct()
-    for s in sums_m:
-        s.through()
     repeat(2, lambda i: grad_columns(2 + i))
     gain_c[c, 0:1] = gain_c[c, 0:1] / gains[0:1, :]
     tell(2, [spot.along(a, by) for a in "xz" for by in (1, -1)])
     gain_got = [wires.send(gain_c.at[c], gain_c.at[c], spot.sibling)]
-    sums_n[1].through()
-    sums_n[2].direct()
-    wires.done(left)
+    for s in sums_n:
+        s.direct()
+    for s in sums_m:
+        s.through()
+
     hear(2, 4)
     att_sum = [
         LineScatter(
@@ -1045,7 +1070,25 @@
     ]
     for line in att_sum:
         line.first()
-    out_sum.second()
+
+    def out_rows_back(r, k):
+        unit = jnp.where(k < 128, k, k - 32)
+        real = (k < 96) | ((k >= 128) & (k < 224))
+        return real & (unit + ((unit * 5462) >> 16) * 4 == r)
+
+    grad_out = dot(mix[...].reshape(8 * OWN, 256), normed[...].reshape(8 * OWN, D), 0, 0)
+    grad_out = dot(picks(256, 256, out_rows_back), grad_out.astype(BF16), 1, 0)
+    wo[...] = grad_out.astype(BF16).reshape(4, 4, 16, D)
+    out_sum = LineScatter(
+        wires, spot, "z",
+        lambda pos, h: wo.at[pos, pl.ds(2 * h, 2)],
+        lambda h: ao.at[0, pl.ds(2 * h, 2)],
+        lambda h: ao.at[1, pl.ds(2 * h, 2)],
+        lambda side, h: ao.at[2 + side, pl.ds(2 * h, 2)],
+    )
+    out_sum.first()
+    for s in sums_n:
+        s.through()
 
     def add_gains(held, axis, into):
         for copy in gain_got:
@@ -1061,15 +1104,9 @@
         return [wires.send(into.at[me], into.at[me], spot.along(axis, by)) for by in (1, -1, 2)]
 
     gain_got = add_gains(gain_c, "x", gain_x)
+    wires.done(left)
     for line in att_sum:
         line.second()
-    sums_n[2].through()
-    dn_sum.finish()
-    dn_got = [
-        wires.send(d_dn.at[turn(y, by), z], dn_in.at[y], spot.along("y", by))
-        for by in (1, -1, 2)
-    ]
-    gain_got = add_gains(gain_x, "z", gain_z)
 
     for copy in gu_got:
         copy.wait_recv()
@@ -1080,6 +1117,8 @@
         other, who = spot.in_quad(by)
         rows = d_gu.at[whole(z * 4 + other, 96), whole(y, 256)]
         gu_done.append(wires.send(rows, gu_own.at[spot.quad], who))
+    gain_got = add_gains(gain_x, "z", gain_z)
+    out_sum.second()
 
     def token_rows(s):
         def use(span):
@@ -1109,40 +1148,47 @@
         s.arrive()
         over_rows(s.start_row, s.size, result_rows(s))
 
-    for s in sums_m:
-        result_part(s)
-    result_kept = wires.move(second.at[c, x], result_out)
-    att_got = []
+    att_got, out_got = [], []
     for line in att_sum:
         line.finish()
-    out_sum.finish()
     for by in (1, -1, 2):
         far, who = turn(z, by), spot.along("z", by)
         att_got.append(wires.send(d_att.at[far, slot, low], att_in.at[z, low], who))
         far, who = slot_of(turn(x, by)), spot.along("x", by)
         att_got.append(wires.send(d_att.at[z, far, high], att_in.at[x, high], who))
-        att_got.append(wires.send(wo.at[z, far], out_in.at[x], who))
+    dn_sum.finish()
+    dn_got = [
+        wires.send(d_dn.at[turn(y, by), z], dn_in.at[y], spot.along("y", by)) for by in (1, -1, 2)
+    ]
     token_part(0)
+    out_sum.finish()
+    for by in (1, -1, 2):
+        far, who = slot_of(turn(x, by)), spot.along("x", by)
+        out_got.append(wires.send(wo.at[z, far], out_in.at[x], who))
+    for s in sums_m:
+        result_part(s)
+    result_kept = wires.move(second.at[c, x], result_out)
     gain_got = add_gains(gain_z, "y", gain_y)
     kept_rows = d_gu.at[whole(z * 4 + spot.quad, 96), whole(y, 256)]
-    gu_out[spot.quad] = kept_rows[...]
+    gu_own[spot.quad] = kept_rows[...]
     for copy in att_got:
         copy.wait_recv()
     for span, me in ((low, z), (high, x)):
         others = [att_in.at[turn(me, by), span] for by in (1, -1, 2)]
         add_into(att_two.at[0, span], d_att.at[z, slot, span], *others)
+    swaps = [wires.send(att_two.at[0], att_two.at[1], spot.partner)]
+    for copy in out_got:
+        copy.wait_recv()
     others = [out_in.at[turn(x, by)] for by in (1, -1, 2)]
     add_into(own_out.at[0], wo.at[z, slot], *others)
-    swaps = [
-        wires.send(att_two.at[0], att_two.at[1], spot.partner),
-        wires.send(own_out.at[0], own_out.at[1], spot.partner),
-    ]
+    swaps.append(wires.send(own_out.at[0], own_out.at[1], spot.partner))
     token_part(1)
     for copy in gu_done:
         copy.wait_recv()
-    for by in (1, 2, 3):
-        other = turn(spot.quad, by)
-        gu_out[other] = gu_own[other]
+    order = picks(512, 512, lambda r, k: quad_order(k) == r)
+    for into, first in ((gate_out, 0), (up_out, 128)):
+        moved = jnp.concatenate([gu_own[i, :, first : first + 128] for i in range(4)], axis=1)
+        into[...] = dot(moved, order, 1, 0)
     for copy in dn_got:
         copy.wait_recv()
     add_into(
@@ -1161,12 +1207,14 @@
 
 
 def finish_kernel(
-    result, token, gains, att, out, gu, dn,
+    result, token, gains, att, out, gate, up, dn,
     result_out, token_out, attn_out, mlp_out, query_out, key_out, value_out, out_out,
     gate_out, up_out, dn_out,
 ):
-    result_out[...] = result[...]
-    token_out[...] = token[...]
+    for src, dst in (
+        (result, result_out), (token, token_out), (gate, gate_out), (up, up_out), (dn, dn_out)
+    ):
+        dst[...] = src[...]
     for i, into in enumerate((attn_out, mlp_out)):
         for j in range(12):
             into[j : j + 1, :] = gains[i : i + 1, j * 128 : j * 128 + 128]
@@ -1179,11 +1227,6 @@
     key_out[...] = dot(rows, picks(384, 96, three(192)), 1, 0)
     value_out[...] = dot(rows, picks(384, 96, three(288)), 1, 0)
     out_out[...] = out[0:12, :].astype(F32)
-    order = picks(512, 512, lambda r, k: quad_order(k) == r)
-    for first, into in ((0, gate_out), (128, up_out)):
-        moved = jnp.concatenate([gu[i, :, first : first + 128] for i in range(4)], axis=1)
-        into[...] = dot(moved, order, 1, 0)
-    dn_out[...] = dn[...]
 
 
 def layer_call(
@@ -1198,7 +1241,8 @@
         (shape((2, D), F32), VMEM),
         (shape((96, 384), BF16), VMEM),
         (shape((16, D), BF16), VMEM),
-        (shape((4, 96, 256), BF16), VMEM),
+        (shape((96, 512), F32), VMEM),
+        (shape((96, 512), F32), VMEM),
         (shape((32, D), F32), VMEM),
     )
     scratch = [
@@ -1278,7 +1322,7 @@
     return pl.pallas_call(
         finish_kernel,
         out_shape=finals,
-        in_specs=[VMEM] * 7,
+        in_specs=[VMEM] * 8,
         out_specs=[VMEM] * 11,
         name="finish",
     )(*outs_raw[1:])

time: 191 us -> 175 us (0.916)
  Pallas kernels: 190 us -> 174 us
    pallas_call x1, Pallas kernels: 187 us -> 171 us  [layer_call(): pl.pallas_call(layer_kernel, out_shape=tuple((o[0] for o in outs)), in_sp...]
where the time goes in v2:
time: 175 us
  Pallas kernels  174 us (99%)
    pallas_call x1, Pallas kernels, layer_call(): pl.pallas_call(layer_kernel, out_shape=tuple((o[0] for o in outs)), in_sp...  171 us

profile of v2, /device:TPU:1, one launch (start us, length us, event | category | flops | bytes accessed | tf_op | source)
XLA Modules:
  0.0 174.5 jit_solution(13444072105686357134)
XLA Ops:
  0.6 170.9 %layer.1 = (bf16[2,4,192,1536]{3,2,1,0:T(8,128)(2,1)}, bf16[192,1536]{1,0:T(8,128)(2,1)}, bf16[192,1536]{1,0:T(8,128)(2,1)}, f32[2,1536]{1,0:T(2,128)}, bf16[96,...) custom-call(bf16[192,1536]{1,0:T(8,128)(2,1)} %tokens.1, ...), custom_call_target="tpu_custom_call" | custom-call | tf_op jit(solution)/shard_map/layer/pallas_call | solution.py:1293
  171.5 3.0 %finish.1 = (bf16[192,1536]{1,0:T(8,128)(2,1)}, bf16[192,1536]{1,0:T(8,128)(2,1)}, f32[12,128]{1,0:T(8,128)}, f32[12,128]{1,0:T(8,128)}, f32[96,192]{1,0:T(8,128...) custom-call(bf16[192,1536]{1,0:T(8,128)(2,1)} %get-tuple-element.30., ...), custom_call_target="tpu_custom_call" | custom-call | tf_op jit(solution)/shard_map/finish/pallas_call | solution.py:1322

commit v3 on v2

--- a/solution.py
+++ b/solution.py
@@ -43,7 +43,7 @@
     def __init__(self):
         x, y, z, c = place()
         self.x, self.y, self.z, self.c = x, y, z, c
-        self.high, self.low = x // 2, x % 2
+        self.high, self.low, self.other = x // 2, x % 2, 1 - c
         self.quad = self.low * 2 + c
         self.sibling = device(x, y, z, 1 - c)
         self.partner = device(turn(x, 2), y, z, 1 - c)
@@ -90,7 +90,11 @@
         self.free.remove(held)
         return held
 
-    def send(self, src, dst, who):
+    def forget(self, copy):
+        self.free += [held for other, held in self.sent if other is copy]
+        self.sent = [pair for pair in self.sent if pair[0] is not copy]
+
+    def send(self, src, dst, who, start=True):
         held = self.take()
         assert self.count < self.recv_sem.shape[0]
         copy = pltpu.make_async_remote_copy(
@@ -102,7 +106,8 @@
             device_id_type=MESH,
         )
         self.count += 1
-        copy.start()
+        if start:
+            copy.start()
         self.sent.append((copy, held))
         return copy
 
@@ -129,6 +134,41 @@
         self.done(self.started())
 
 
+class Placed:
+    def __init__(self, wires, stays, pieces):
+        self.wires, self.stays = wires, stays
+        self.others = [wires.send(*piece) for piece in pieces[1:]]
+        self.own = wires.send(*pieces[0], start=False)
+        held = wires.sent[-1][1]
+
+        @pl.when(jnp.logical_not(stays))
+        def _():
+            self.own.start()
+
+        @pl.when(stays)
+        def _():
+            kept = pltpu.make_async_copy(pieces[0][0], pieces[0][1], wires.send_sem.at[held])
+            kept.start()
+            kept.wait()
+
+    def wait(self):
+        for copy in self.others:
+            copy.wait_recv()
+
+        @pl.when(jnp.logical_not(self.stays))
+        def _():
+            self.own.wait_recv()
+
+    def close(self):
+        self.wires.done(self.others)
+
+        @pl.when(jnp.logical_not(self.stays))
+        def _():
+            self.own.wait_send()
+
+        self.wires.forget(self.own)
+
+
 class Moved:
     def __init__(self, wires, copy, held):
         self.wires, self.copy, self.held = wires, copy, held
@@ -260,11 +300,12 @@
             return pl.ds(self.start_row, self.size)
         return pl.ds(self.start_row + half * self.cut, self.cut)
 
-    def share(self):
+    def share(self, start=True):
         self.shared = self.wires.send(
-            self.part.at[1 - self.spot.c, :, self.rows()],
+            self.part.at[self.spot.other, :, self.rows()],
             self.got.at[:, self.rows()],
             self.spot.sibling,
+            start,
         )
 
     def first(self):
@@ -332,11 +373,17 @@
         self.next, self.prev = spot.along(axis, 1), spot.along(axis, -1)
         self.passed, self.work, self.near = passed, work, near
 
-    def first(self):
+    def first(self, paced=False):
         send, me = self.wires.send, self.me
-        far, after, before = turn(me, 2), turn(me, 1), turn(me, -1)
+        far = turn(me, 2)
         self.pass0 = send(self.at(far, 0), self.passed(0), self.next)
         self.pass1 = send(self.at(far, 1), self.passed(1), self.prev)
+        if not paced:
+            self.direct()
+
+    def direct(self):
+        send, me = self.wires.send, self.me
+        after, before = turn(me, 1), turn(me, -1)
         self.arriving = [
             send(self.at(after, 1), self.near(0, 1), self.next),
             send(self.at(before, 0), self.near(1, 0), self.prev),
@@ -447,6 +494,8 @@
         + [spot.along(a, 2) for a in "xyz"]
         + [spot.partner]
         + [spot.in_quad(by)[1] for by in (1, 2, 3)]
+        + [device(turn(x, by), y, z, 1 - c) for by in (1, -1)]
+        + [device(turn(x, 2), y, turn(z, by), 1 - c) for by in (1, -1, 2)]
     )
     greet(neighbours)
 
@@ -479,13 +528,28 @@
     own_out[0, 0:12] = w_out[...]
     greeted(neighbours)
 
-    swaps = [
-        wires.send(att_two.at[0], att_two.at[1], spot.partner),
-        wires.send(own_out.at[0], own_out.at[1], spot.partner),
+    def slot_of(pos):
+        return (pos % 2) * 2 + pos // 2
+
+    slot = slot_of(x)
+    low, high = pl.ds(0, 48), pl.ds(48, 48)
+    stays = spot.high == c
+    there_x, there_c = jnp.where(stays, x, turn(x, 2)), jnp.where(stays, c, 1 - c)
+    there = slot_of(there_x)
+    line_z = [device(there_x, y, turn(z, by), there_c) for by in (0, 1, -1, 2)]
+    line_x = [device(turn(there_x, by), y, z, there_c) for by in (0, 1, -1, 2)]
+    att_side = [
+        Placed(
+            wires, stays, [(att_two.at[0, low], aq.at[z, there, low], who) for who in line_z]
+        ),
+        Placed(
+            wires, stays, [(att_two.at[0, high], aq.at[z, there, high], who) for who in line_x]
+        ),
     ]
     rows_y = [PairGather(wires, spot, "y", normed, own, s, n) for s, n in TWO]
     for g in rows_y:
         g.start()
+    out_side = Placed(wires, stays, [(own_out.at[0], ao.at[z, there], who) for who in line_x])
     marks_kept = wires.move(marks, marks_two.at[c])
     marks_got = wires.send(marks, marks_two.at[c], spot.sibling)
 
@@ -524,29 +588,6 @@
 
     marks_kept.wait()
     trig(c)
-    for copy in swaps:
-        copy.wait_recv()
-
-    def slot_of(pos):
-        return (pos % 2) * 2 + pos // 2
-
-    slot = slot_of(x)
-    pick = jnp.where(spot.high == c, 0, 1)
-    low, high = pl.ds(0, 48), pl.ds(48, 48)
-    att_kept = [
-        wires.move(att_two.at[pick], aq.at[z, slot]),
-        wires.move(own_out.at[pick], ao.at[z, slot]),
-    ]
-    att_side, out_side = [], []
-    for by in (1, -1, 2):
-        att_side.append(
-            wires.send(att_two.at[pick, low], aq.at[z, slot, low], spot.along("z", by))
-        )
-        att_side.append(
-            wires.send(att_two.at[pick, high], aq.at[z, slot, high], spot.along("x", by))
-        )
-    for by in (1, -1, 2):
-        out_side.append(wires.send(own_out.at[pick], ao.at[z, slot], spot.along("x", by)))
     for g in rows_y:
         g.rest()
     att_line = [
@@ -555,21 +596,18 @@
     ]
     out_line = RingGather(wires, spot, "z", lambda pos, h: ao.at[pos, pl.ds(2 * h, 2)])
     cot_x = [PairGather(wires, spot, "x", cots, cot, s, n) for s, n in TWO]
+    for piece in att_side:
+        piece.wait()
+    for line in att_line:
+        line.begin()
     marks_got.wait_recv()
     trig(1 - c)
-    for copy in att_kept:
-        copy.wait()
-    for copy in att_side:
-        copy.wait_recv()
-    for line in att_line:
-        line.begin()
     for g in rows_y:
         g.forward()
     rows_y[0].near()
     for line in att_line:
         line.forward()
-    for copy in out_side:
-        copy.wait_recv()
+    out_side.wait()
     out_line.begin()
     dn_here = dn.at[y, z]
     dn_kept = wires.move(w_down, dn_here)
@@ -592,6 +630,8 @@
         real = (r < 96) | ((r >= 128) & (r < 224))
         return real & (unit + ((unit * 5462) >> 16) * 4 == k)
 
+    scale = HD ** (-0.5)
+
     def project(core, pos):
         both = dot(normed[core, pos], aq[...].reshape(D, 384), 1, 0)
         span = whole(pos, OWN)
@@ -599,12 +639,13 @@
         tile = [both[:, 128 * i : 128 * i + 128] for i in range(3)]
         lane = lax.broadcasted_iota(jnp.int32, tile[0].shape, 1)
 
-        def turned(values):
-            return (values * cos + swap_halves(values) * sin).astype(BF16)
-
-        q[core, span, 0:128] = turned(tile[0])
+        def turned(values, factor=None):
+            values = values * cos + swap_halves(values) * sin
+            return (values if factor is None else values * factor).astype(BF16)
+
+        q[core, span, 0:128] = turned(tile[0], scale)
         q[core, span, 128:256] = turned(
-            jnp.where(lane < 32, pltpu.roll(tile[0], 32, 1), pltpu.roll(tile[1], 32, 1))
+            jnp.where(lane < 32, pltpu.roll(tile[0], 32, 1), pltpu.roll(tile[1], 32, 1)), scale
         )
         after = pl.ds(pl.multiple_of(WIN + pos * OWN, 64), OWN)
         kv[core, after, 0:128] = turned(
@@ -632,42 +673,12 @@
     gu_side.begin()
     out_line.forward()
     project(c, turn(y, 2))
-    for g in rows_y:
-        g.shared[3].wait_recv()
-    project(1 - c, turn(y, 2))
-    kv_got = wires.send(kv.at[:, pl.ds(768, WIN)], kv.at[:, pl.ds(0, WIN)], spot.along("x", 2))
-    normed_kept = wires.move(normed, normed_out)
-    left = wires.started()
-    cot_x[0].forward()
-    cot_x[0].near()
-    gu_line = RingGather(
-        wires, spot, "z", lambda pos, h: gu.at[whole(pos, 384), pl.ds(h * 512, 512)]
-    )
-
-    scale = HD ** (-0.5)
-
-    def attend(core, run, head):
-        span = whole(run, WIN)
-        lanes = whole(head, 128)
-        window = pl.ds(pl.multiple_of(run * WIN, WIN), SEQ)
-        scores = dot(q[core, span, lanes], kv[core, window, 0:128], 1, 1) * scale
-        row, column = grid_of(WIN, SEQ)
-        spot_of = spot.high * HALF + run * WIN + row[:, 0:1]
-        begin = jnp.maximum(
-            (spot_of >> 9) << 9, spot_of - grad_kv[core, span, 0:1].astype(jnp.int32)
-        )
-        begin = begin - (spot.high * HALF + run * WIN) + WIN
-        allowed = (column >= begin) & (column <= row + WIN)
-        scores = jnp.where(allowed, scores, MASKED)
-        weights = jnp.exp(scores - jnp.max(scores, axis=-1, keepdims=True))
-        share = weights / jnp.sum(weights, axis=-1, keepdims=True)
-        rounded = share.astype(BF16)
-        prob[core, run, head] = rounded
-        values = dot(rounded, kv[core, window, 128:256], 1, 0)
-        mix[core, span, lanes] = values.astype(BF16)
-
-    repeat(4, lambda i: attend(i // 2, 1, i % 2))
-    gu_side.forward()
+
+    def send_kv(core):
+        last, first = kv.at[core, pl.ds(768, WIN)], kv.at[core, pl.ds(0, WIN)]
+        return wires.send(last, first, spot.along("x", 2))
+
+    kv_got = [send_kv(c)]
     dn_kept.wait()
     for copy in dn_side:
         copy.wait_recv()
@@ -675,9 +686,51 @@
         RingGather(wires, spot, "y", lambda pos, h: dn.at[pos, pl.ds(2 * h, 2), first_rows]),
         RingGather(wires, spot, "z", lambda pos, h: dn.at[pl.ds(2 * h, 2), pos, last_rows]),
     ]
-    for line in dn_line:
-        line.begin()
-    repeat(4, lambda i: attend(i // 2, 2, i % 2))
+    dn_line[1].begin()
+    for g in rows_y:
+        g.shared[3].wait_recv()
+    project(1 - c, turn(y, 2))
+    kv_got.append(send_kv(1 - c))
+    normed_kept = wires.move(normed, normed_out)
+    for piece in att_side + [out_side]:
+        piece.close()
+    left = wires.started()
+    cot_x[0].forward()
+    cot_x[0].near()
+    gu_line = RingGather(
+        wires, spot, "z", lambda pos, h: gu.at[whole(pos, 384), pl.ds(h * 512, 512)]
+    )
+
+    def both_heads(ref, core, span):
+        return jnp.concatenate([ref[core, span, 0:128], ref[core, span, 128:256]], axis=0)
+
+    def attend(core, run):
+        span = pl.ds(run * WIN, WIN)
+        window = pl.ds(run * WIN, SEQ)
+        scores = dot(both_heads(q, core, span), kv[core, window, 0:128], 1, 1)
+        row, column = grid_of(2 * WIN, SEQ)
+        row = row & (WIN - 1)
+        spot_of = spot.high * HALF + run * WIN + row[0:WIN, 0:1]
+        begin = jnp.maximum(
+            (spot_of >> 9) << 9, spot_of - grad_kv[core, span, 0:1].astype(jnp.int32)
+        )
+        begin = begin - (spot.high * HALF + run * WIN) + WIN
+        begin = jnp.concatenate([begin, begin], axis=0)
+        allowed = (column >= begin) & (column <= row + WIN)
+        scores = jnp.where(allowed, scores, MASKED)
+        weights = jnp.exp(scores - jnp.max(scores, axis=-1, keepdims=True))
+        share = weights * (1.0 / jnp.sum(weights, axis=-1, keepdims=True))
+        rounded = share.astype(BF16)
+        prob[core, run] = rounded
+        values = dot(rounded, kv[core, window, 128:256], 1, 0).astype(BF16)
+        mix[core, span, 0:128] = values[0:WIN]
+        mix[core, span, 128:256] = values[WIN : 2 * WIN]
+
+    repeat(2, lambda i: attend(i, 1))
+    gu_side.forward()
+    dn_line[0].begin()
+    repeat(2, lambda i: attend(i, 2))
+    dn_line[1].forward()
     out_line.near()
     out_line.far()
     out_rows = picks(256, 256, out_row)
@@ -692,25 +745,28 @@
         for s in sums:
             s.share()
 
-    def back_hidden(s):
+    def back_hidden(i):
+        start, size = THREE[i]
+
         def step(core):
-            rows = cots[core, :, pl.ds(s * 64, 64)].reshape(256, D)
-            grad_hidden[core * 3 + s] = dot(rows, dn[...].reshape(512, D), 1, 1).astype(BF16)
+            rows = cots[core, :, pl.ds(start, size)].reshape(4 * size, D)
+            grad = dot(rows, dn[...].reshape(512, D), 1, 1).astype(BF16)
+            grad_hidden[core, pl.ds(4 * start, 4 * size)] = grad
 
         repeat(2, step)
 
     sums_y = [PairScatter(wires, spot, "y", part, got, passed, near, s, n) for s, n in THREE]
     rows_x = [PairGather(wires, spot, "x", second, own, s, n) for s, n in THREE]
     repeat(2, lambda i: project_out(i, 1))
+    for copy in kv_got:
+        copy.wait_recv()
+    cot_x[1].start()
     gu_side.near()
     gu_side.far()
     gu_line.start()
-    kv_got.wait_recv()
-    cot_x[1].start()
-    repeat(4, lambda i: attend(i // 2, 0, i % 2))
+    repeat(2, lambda i: attend(i, 0))
     cot_x[1].rest()
-    for line in dn_line:
-        line.forward()
+    dn_line[0].forward()
     project_out(1 - c, 0)
     sums_y[0].share()
     project_out(c, 0)
@@ -776,11 +832,11 @@
     rows_x[0].finish()
 
     def feed(core, i):
-        span = pl.ds(*THREE[i])
-        size = 4 * THREE[i][1]
+        start, part_size = THREE[i]
+        span, size = pl.ds(start, part_size), 4 * part_size
         rows = second[core, :, span].reshape(size, D)
         both = dot(rows, gu[...], 1, 0)
-        upstream = grad_hidden[core * 3 + i].astype(F32)
+        upstream = grad_hidden[core, pl.ds(4 * start, size)].astype(F32)
         for j in range(4):
             gate = both[:, j * 256 : j * 256 + 128]
             upward = both[:, j * 256 + 128 : j * 256 + 256]
@@ -793,44 +849,29 @@
                 (j * 256, sent * upward * slope),
                 (j * 256 + 128, sent * silu),
             ):
-                rounded = values.astype(BF16).reshape(4, THREE[i][1], 128)
+                rounded = values.astype(BF16).reshape(4, part_size, 128)
                 work[core, :, span, first : first + 128] = rounded
         back = dot(work[core, :, span, 0:1024].reshape(size, 1024), gu[...], 1, 1)
-        part[core, :, span] = back.astype(BF16).reshape(4, THREE[i][1], D)
+        part[core, :, span] = back.astype(BF16).reshape(4, part_size, D)
 
     sums_x = [PairScatter(wires, spot, "x", part, got, passed, near, s, n) for s, n in THREE]
     grads_y = [PairGather(wires, spot, "y", normed, own, s, n) for s, n in THREE]
 
-    def feed_share(i):
-        feed(1 - c, i)
-        sums_x[i].share()
+    def feed_both(i):
+        sums_x[i].share(start=False)
+
+        def step(k):
+            feed(jnp.where(k == 0, spot.other, c), i)
+
+            @pl.when(k == 0)
+            def _():
+                sums_x[i].shared.start()
+
+        repeat(2, step)
 
     gather_next(2)
     early = wires.started()
     wires.again()
-    feed_share(0)
-    rows_x[2].rest()
-    rows_x[1].near()
-    feed(c, 0)
-    rows_x[2].forward()
-    sums_x[0].first()
-    rows_x[1].far()
-    sums_x[0].direct()
-    rows_x[1].finish()
-    rows_x[2].near()
-    feed_share(1)
-    rows_x[2].far()
-    feed(c, 1)
-    sums_x[1].first()
-    sums_x[0].through()
-    rows_x[2].finish()
-    sums_x[1].direct()
-    feed_share(2)
-    feed(c, 2)
-    sums_x[2].first()
-    sums_x[1].through()
-    wires.done(early)
-    tell(0, [spot.along("z", 1), spot.along("z", -1)])
 
     def grad_gate_up(i):
         lanes = whole(i, 256)
@@ -871,27 +912,51 @@
         grads_y[i].start()
 
     def mix_back(i):
+        first, size = THREE[i]
+
         def step(core):
-            span = pl.ds(*THREE[i])
-            rows = normed[core, :, span].reshape(256, D)
+            rows = normed[core, :, pl.ds(first, size)].reshape(4 * size, D)
             grad = dot(rows, wo[...].reshape(256, D), 1, 1).astype(BF16)
             for pos in range(4):
-                start = pos * OWN + THREE[i][0]
-                grad_mix[core, start : start + 64, :] = grad[pos * 64 : pos * 64 + 64]
+                start = pos * OWN + first
+                grad_mix[core, start : start + size, :] = grad[pos * size : pos * size + size]
 
         repeat(2, step)
 
     total[...] = jnp.zeros_like(total)
+
+    feed_both(0)
+    rows_x[2].rest()
+    rows_x[2].forward()
+    rows_x[1].near()
+    rows_x[1].far()
+    sums_x[0].first()
+    rows_x[1].finish()
+    feed_both(1)
+    rows_x[2].near()
+    sums_x[0].direct()
+    rows_x[2].far()
+    sums_x[0].through()
+    sums_x[1].first()
+    rows_x[2].finish()
+    sums_x[1].direct()
+    feed_both(2)
+    sums_x[2].first()
     gather_back(0)
+    sums_x[1].through()
     sums_x[2].direct()
+    wires.done(early)
+    tell(0, [spot.along("z", 1), spot.along("z", -1)])
+
+    grads_y[0].rest()
     repeat(2, grad_gate_up)
-    grads_y[0].rest()
+    grads_y[0].forward()
     repeat(2, lambda i: grad_gate_up(2 + i))
+    sums_x[2].through()
     gather_back(1)
-    grads_y[0].forward()
-    sums_x[2].through()
+    grads_y[0].near()
+    repeat(2, lambda i: grad_gate_up(4 + i))
     grads_y[1].rest()
-    repeat(2, lambda i: grad_gate_up(4 + i))
     hear(0, 2)
     gu_sum = [
         LineScatter(
@@ -913,25 +978,24 @@
             gu_got.append(wires.send(part_of, into, spot.along("y", by)))
 
     gu_sum[0].first()
-    grads_y[0].near()
+    grads_y[0].far()
+    gather_back(2)
     grads_y[1].forward()
-    gather_back(2)
-    grads_y[0].far()
     grad_down(0)
     grads_y[2].rest()
-    grads_y[1].near()
-    repeat(2, down)
-    grads_y[2].forward()
     grads_y[0].finish()
     mix_back(0)
+    grads_y[1].near()
+    grads_y[2].forward()
     gu_sum[0].second()
     gu_sum[1].first()
+    grad_down(1)
     grads_y[1].far()
-    grad_down(1)
     grads_y[2].near()
+    repeat(2, down)
+    grads_y[2].far()
     grads_y[1].finish()
     mix_back(1)
-    grads_y[2].far()
     repeat(2, lambda i: down(2 + i))
     tell(1, around(spot, "xy") + [spot.along("z", 1), spot.along("z", -1)])
     again = wires.move(normed_out, cots)
@@ -940,29 +1004,33 @@
     mix_back(2)
     left = wires.started()
 
-    def attend_back(core, run, head):
-        span = whole(run, WIN)
-        lanes = whole(head, 128)
-        window = pl.ds(pl.multiple_of(run * WIN, WIN), SEQ)
-        rounded = prob[core, run, head]
-        share = rounded.astype(F32)
-        mixed = grad_mix[core, span, lanes]
-        asked = q[core, span, lanes]
+    def attend_back(core, run):
+        span = pl.ds(run * WIN, WIN)
+        window = pl.ds(run * WIN, SEQ)
+        rounded = prob[core, run]
+        mixed = both_heads(grad_mix, core, span)
+        inner = mixed.astype(F32) * both_heads(mix, core, span).astype(F32)
+        inner = jnp.sum(inner, axis=-1, keepdims=True)
         grad = dot(mixed, kv[core, window, 128:256], 1, 1)
-        inner = jnp.sum(share * grad, axis=-1, keepdims=True)
-        scored = (share * (grad - inner)).astype(BF16)
-        grad_kv[core, window, 0:128] += dot(scored, asked, 0, 0) * scale
+        scored = (rounded.astype(F32) * (grad - inner)).astype(BF16)
+        grad_kv[core, window, 0:128] += dot(scored, both_heads(q, core, span), 0, 0)
         grad_kv[core, window, 128:256] += dot(rounded, mixed, 0, 0)
         grad_q = dot(scored, kv[core, window, 0:128], 1, 0) * scale
         cos, sin = cosine[core, span, :], sine[core, span, :]
-        q[core, span, lanes] = (grad_q * cos - swap_halves(grad_q) * sin).astype(BF16)
-
-    repeat(4, lambda i: attend_back(i // 2, 0, i % 2))
-    far_from = grad_mix.at[:, pl.ds(0, WIN)]
+        for head in (0, 1):
+            grad = grad_q[head * WIN : head * WIN + WIN]
+            grad = (grad * cos - swap_halves(grad) * sin).astype(BF16)
+            q[core, span, head * 128 : head * 128 + 128] = grad
+
+    def send_far(core):
+        far_from = grad_mix.at[core, pl.ds(0, WIN)]
+        far_from[...] = grad_kv[core, 0:WIN, :].astype(BF16)
+        return wires.send(far_from, far_kv.at[core], spot.along("x", 2))
+
+    far_got = []
     for core in (0, 1):
-        far_from[core] = grad_kv[core, 0:WIN, :].astype(BF16)
-    far_got = wires.send(far_from, far_kv, spot.along("x", 2))
-    gu_sum[1].second()
+        attend_back(core, 0)
+        far_got.append(send_far(core))
     gu_beside(0)
     hear(1, 7)
     sums_m = [
@@ -971,11 +1039,13 @@
         )
         for s, n in TWO
     ]
-    share_all(sums_m)
-    repeat(4, lambda i: attend_back(i // 2, 1, i % 2))
+    sums_m[0].share()
+    gu_sum[1].second()
+    repeat(2, lambda i: attend_back(i, 1))
     sums_m[0].first()
     sums_m[0].direct()
-    repeat(4, lambda i: attend_back(i // 2, 2, i % 2))
+    sums_m[1].share()
+    repeat(2, lambda i: attend_back(i, 2))
     sums_m[1].first()
     sums_m[1].direct()
     dn_sum = LineScatter(
@@ -986,12 +1056,8 @@
         lambda side, h: dn.at[2 + side, pl.ds(2 * h, 2)],
     )
     dn_sum.first()
-    far_got.wait_recv()
-    for core in (0, 1):
-        grad_kv[core, 768:1024, :] += far_kv[core].astype(F32)
-
-    def turn_back(i):
-        core, pos = i // 4, i % 4
+
+    def turn_back(core, pos):
         after = pl.ds(pl.multiple_of(WIN + pos * OWN, 64), OWN)
         span = whole(pos, OWN)
         cos, sin = cosine[core, span, :], sine[core, span, :]
@@ -1005,23 +1071,29 @@
         q[core, span, 128:256] = jnp.where(lane < 64, behind, keyed).astype(BF16)
         kv[core, after, 0:128] = jnp.where(lane < 32, keyed, valued).astype(BF16)
 
-    repeat(8, turn_back)
+
+    def normed_back(core, half):
+        after = pl.ds(WIN + half * 384, 384)
+        span = pl.ds(half * 384, 384)
+        rows = jnp.concatenate([q[core, span, :], kv[core, after, 0:128]], axis=1)
+        grad = dot(rows, aq[...].reshape(D, 384), 1, 1).astype(BF16)
+        part[core, half * 2 : half * 2 + 2] = grad.reshape(2, OWN, D)
+
+    sums_n = [PairScatter(wires, spot, "y", part, got, passed, near, s, n) for s, n in THREE]
     gu_beside(1)
-
-    def normed_back(core):
-        def step(pos):
-            after = pl.ds(pl.multiple_of(WIN + pos * 384, 128), 384)
-            rows = jnp.concatenate([q[core, whole(pos, 384), :], kv[core, after, 0:128]], axis=1)
-            grad = dot(rows, aq[...].reshape(D, 384), 1, 1).astype(BF16)
-            part[core, pl.ds(pos * 2, 2)] = grad.reshape(2, OWN, D)
-
-        repeat(2, step)
-
-    sums_n = [PairScatter(wires, spot, "y", part, got, passed, near, s, n) for s, n in THREE]
-    normed_back(1 - c)
+    repeat(4, lambda i: turn_back(i // 2, i % 2))
+    repeat(2, lambda i: normed_back(i, 0))
+    for copy in far_got:
+        copy.wait_recv()
+    for core in (0, 1):
+        grad_kv[core, 768:1024, :] += far_kv[core].astype(F32)
+    repeat(4, lambda i: turn_back(i // 2, 2 + i % 2))
+    normed_back(1 - c, 1)
     share_all(sums_n)
-    normed_back(c)
+    normed_back(c, 1)
     sums_n[0].first()
+    sums_n[1].first()
+    sums_n[2].first()
     dn_sum.second()
     again.wait()
 
@@ -1039,10 +1111,7 @@
         )
         gain_c[c, 0:1, whole(i, 384)] = jnp.sum(folded.T, axis=0, keepdims=True)
 
-    repeat(2, grad_columns)
-    sums_n[1].first()
-    sums_n[2].first()
-    repeat(2, lambda i: grad_columns(2 + i))
+    repeat(4, grad_columns)
     gain_c[c, 0:1] = gain_c[c, 0:1] / gains[0:1, :]
     tell(2, [spot.along(a, by) for a in "xz" for by in (1, -1)])
     gain_got = [wires.send(gain_c.at[c], gain_c.at[c], spot.sibling)]
@@ -1051,6 +1120,21 @@
     for s in sums_m:
         s.through()
 
+    def out_rows_back(r, k):
+        unit = jnp.where(k < 128, k, k - 32)
+        real = (k < 96) | ((k >= 128) & (k < 224))
+        return real & (unit + ((unit * 5462) >> 16) * 4 == r)
+
+    grad_out = dot(mix[...].reshape(8 * OWN, 256), normed[...].reshape(8 * OWN, D), 0, 0)
+    grad_out = dot(picks(256, 256, out_rows_back), grad_out.astype(BF16), 1, 0)
+    wo[...] = grad_out.astype(BF16).reshape(4, 4, 16, D)
+    out_sum = LineScatter(
+        wires, spot, "z",
+        lambda pos, h: wo.at[pos, pl.ds(2 * h, 2)],
+        lambda h: ao.at[0, pl.ds(2 * h, 2)],
+        lambda h: ao.at[1, pl.ds(2 * h, 2)],
+        lambda side, h: ao.at[2 + side, pl.ds(2 * h, 2)],
+    )
     hear(2, 4)
     att_sum = [
         LineScatter(
@@ -1068,25 +1152,9 @@
             lambda side, h: aq.at[2 + side, pl.ds(2 * h, 2), high],
         ),
     ]
-    for line in att_sum:
-        line.first()
-
-    def out_rows_back(r, k):
-        unit = jnp.where(k < 128, k, k - 32)
-        real = (k < 96) | ((k >= 128) & (k < 224))
-        return real & (unit + ((unit * 5462) >> 16) * 4 == r)
-
-    grad_out = dot(mix[...].reshape(8 * OWN, 256), normed[...].reshape(8 * OWN, D), 0, 0)
-    grad_out = dot(picks(256, 256, out_rows_back), grad_out.astype(BF16), 1, 0)
-    wo[...] = grad_out.astype(BF16).reshape(4, 4, 16, D)
-    out_sum = LineScatter(
-        wires, spot, "z",
-        lambda pos, h: wo.at[pos, pl.ds(2 * h, 2)],
-        lambda h: ao.at[0, pl.ds(2 * h, 2)],
-        lambda h: ao.at[1, pl.ds(2 * h, 2)],
-        lambda side, h: ao.at[2 + side, pl.ds(2 * h, 2)],
-    )
-    out_sum.first()
+    for line in att_sum + [out_sum]:
+        line.first(paced=True)
+
     for s in sums_n:
         s.through()
 
@@ -1104,10 +1172,12 @@
         return [wires.send(into.at[me], into.at[me], spot.along(axis, by)) for by in (1, -1, 2)]
 
     gain_got = add_gains(gain_c, "x", gain_x)
+    for line in att_sum + [out_sum]:
+        line.direct()
     wires.done(left)
-    for line in att_sum:
+
+    for line in att_sum + [out_sum]:
         line.second()
-
     for copy in gu_got:
         copy.wait_recv()
     mine = d_gu.at[whole(z, 384), whole(y, 256)]
@@ -1118,7 +1188,6 @@
         rows = d_gu.at[whole(z * 4 + other, 96), whole(y, 256)]
         gu_done.append(wires.send(rows, gu_own.at[spot.quad], who))
     gain_got = add_gains(gain_x, "z", gain_z)
-    out_sum.second()
 
     def token_rows(s):
         def use(span):
@@ -1148,41 +1217,41 @@
         s.arrive()
         over_rows(s.start_row, s.size, result_rows(s))
 
-    att_got, out_got = [], []
-    for line in att_sum:
-        line.finish()
-    for by in (1, -1, 2):
-        far, who = turn(z, by), spot.along("z", by)
-        att_got.append(wires.send(d_att.at[far, slot, low], att_in.at[z, low], who))
-        far, who = slot_of(turn(x, by)), spot.along("x", by)
-        att_got.append(wires.send(d_att.at[z, far, high], att_in.at[x, high], who))
     dn_sum.finish()
     dn_got = [
         wires.send(d_dn.at[turn(y, by), z], dn_in.at[y], spot.along("y", by)) for by in (1, -1, 2)
     ]
-    token_part(0)
-    out_sum.finish()
-    for by in (1, -1, 2):
-        far, who = slot_of(turn(x, by)), spot.along("x", by)
-        out_got.append(wires.send(wo.at[z, far], out_in.at[x], who))
     for s in sums_m:
         result_part(s)
     result_kept = wires.move(second.at[c, x], result_out)
+    for line in att_sum:
+        line.finish()
+
+    def home(pos):
+        stay = pos // 2 == c
+        return device(jnp.where(stay, pos, turn(pos, 2)), y, z, jnp.where(stay, c, 1 - c))
+
+    places_z = [(turn(z, by), who) for by, who in zip((0, 1, -1, 2), line_z)]
+    places_x = [turn(x, by) for by in (0, 1, -1, 2)]
+    att_got = [
+        Placed(
+            wires, stays, [(d_att.at[to, slot, low], att_in.at[z, low], w) for to, w in places_z]
+        ),
+        Placed(
+            wires, stays,
+            [(d_att.at[z, slot_of(to), high], att_in.at[x, high], home(to)) for to in places_x],
+        ),
+    ]
+    out_sum.finish()
+    out_got = Placed(
+        wires, stays, [(wo.at[z, slot_of(to)], out_in.at[x], home(to)) for to in places_x]
+    )
     gain_got = add_gains(gain_z, "y", gain_y)
     kept_rows = d_gu.at[whole(z * 4 + spot.quad, 96), whole(y, 256)]
     gu_own[spot.quad] = kept_rows[...]
-    for copy in att_got:
-        copy.wait_recv()
-    for span, me in ((low, z), (high, x)):
-        others = [att_in.at[turn(me, by), span] for by in (1, -1, 2)]
-        add_into(att_two.at[0, span], d_att.at[z, slot, span], *others)
-    swaps = [wires.send(att_two.at[0], att_two.at[1], spot.partner)]
-    for copy in out_got:
-        copy.wait_recv()
-    others = [out_in.at[turn(x, by)] for by in (1, -1, 2)]
-    add_into(own_out.at[0], wo.at[z, slot], *others)
-    swaps.append(wires.send(own_out.at[0], own_out.at[1], spot.partner))
+    token_part(0)
     token_part(1)
+    token_part(2)
     for copy in gu_done:
         copy.wait_recv()
     order = picks(512, 512, lambda r, k: quad_order(k) == r)
@@ -1194,15 +1263,17 @@
     add_into(
         dn_out, d_dn.at[y, z], *[dn_in.at[turn(y, by)] for by in (1, -1, 2)]
     )
-    token_part(2)
+    for piece in att_got:
+        piece.wait()
+    add_into(att_out, *[att_in.at[i] for i in range(4)])
+    out_got.wait()
+    add_into(out_out, *[out_in.at[i] for i in range(4)])
     add_gains(gain_y, None, None)
-    for copy in swaps:
-        copy.wait_recv()
-    att_out[...] = att_two[pick]
-    out_out[...] = own_out[pick]
     result_kept.wait()
     for copy in token_kept:
         copy.wait()
+    for piece in att_got + [out_got]:
+        piece.close()
     wires.close()
 
 
@@ -1254,8 +1325,8 @@
         ((OWN, D), BF16),
         ((2, OWN, D), BF16),
         ((2, 4, OWN, D), BF16),
-        ((2, 96, 384), BF16),
-        ((2, 16, D), BF16),
+        ((1, 96, 384), BF16),
+        ((1, 16, D), BF16),
         ((4, 4, 96, 384), BF16),
         ((4, 4, 16, D), BF16),
         ((4, 4, 96, 384), BF16),
@@ -1266,10 +1337,10 @@
         ((D, 1024), BF16),
         ((4, 4, 32, D), BF16),
         ((OWN, D), BF16),
-        ((6, 256, 512), BF16),
+        ((2, 4 * OWN, 512), BF16),
         ((2, HALF, 256), BF16),
         ((2, HALF + WIN, 256), BF16),
-        ((2, 3, 2, WIN, SEQ), BF16),
+        ((2, 3, 2 * WIN, SEQ), BF16),
         ((2, HALF, 256), BF16),
         ((2, HALF, 128), F32),
         ((2, HALF, 128), F32),

time: 175 us -> 171 us (0.977)
  Pallas kernels: 174 us -> 170 us
    pallas_call x1, Pallas kernels: 171 us -> 167 us  [layer_call(): pl.pallas_call(layer_kernel, out_shape=tuple((o[0] for o in outs)), in_sp...]
where the time goes in v3:
time: 171 us
  Pallas kernels  170 us (99%)
    pallas_call x1, Pallas kernels, layer_call(): pl.pallas_call(layer_kernel, out_shape=tuple((o[0] for o in outs)), in_sp...  167 us

profile of v3, /device:TPU:1, one launch (start us, length us, event | category | flops | bytes accessed | tf_op | source)
XLA Modules:
  0.0 170.6 jit_solution(3719016585958772735)
XLA Ops:
  0.6 166.9 %layer.1 = (bf16[2,4,192,1536]{3,2,1,0:T(8,128)(2,1)}, bf16[192,1536]{1,0:T(8,128)(2,1)}, bf16[192,1536]{1,0:T(8,128)(2,1)}, f32[2,1536]{1,0:T(2,128)}, bf16[96,...) custom-call(bf16[192,1536]{1,0:T(8,128)(2,1)} %tokens.1, ...), custom_call_target="tpu_custom_call" | custom-call | tf_op jit(solution)/shard_map/layer/pallas_call | solution.py:1364
  167.5 3.0 %finish.1 = (bf16[192,1536]{1,0:T(8,128)(2,1)}, bf16[192,1536]{1,0:T(8,128)(2,1)}, f32[12,128]{1,0:T(8,128)}, f32[12,128]{1,0:T(8,128)}, f32[96,192]{1,0:T(8,128...) custom-call(bf16[192,1536]{1,0:T(8,128)(2,1)} %get-tuple-element.30., ...), custom_call_target="tpu_custom_call" | custom-call | tf_op jit(solution)/shard_map/finish/pallas_call | solution.py:1393

commit v4 on v3

--- a/solution.py
+++ b/solution.py
@@ -294,22 +294,26 @@
         self.next, self.prev = spot.along(axis, 1), spot.along(axis, -1)
         self.part, self.got, self.passed, self.near = part, got, passed, near
         self.start_row, self.size, self.cut = start, size, size // 2
+        self.shared = []
 
     def rows(self, half=None):
         if half is None:
             return pl.ds(self.start_row, self.size)
         return pl.ds(self.start_row + half * self.cut, self.cut)
 
-    def share(self, start=True):
-        self.shared = self.wires.send(
-            self.part.at[self.spot.other, :, self.rows()],
-            self.got.at[:, self.rows()],
+    def share(self, half=None, start=True):
+        places = slice(None) if half is None else pl.ds(half * 2, 2)
+        copy = self.wires.send(
+            self.part.at[self.spot.other, places, self.rows()],
+            self.got.at[places, self.rows()],
             self.spot.sibling,
             start,
         )
+        self.shared = (self.shared if half is not None else []) + [copy]
 
     def first(self):
-        self.shared.wait_recv()
+        for copy in self.shared:
+            copy.wait_recv()
         pos = turn(self.me, 2)
         mine = self.got.at[pos, self.rows()]
         add_into(mine, self.part.at[self.spot.c, pos, self.rows()], mine)
@@ -355,7 +359,7 @@
             copy.wait_recv()
 
     def close(self):
-        self.wires.done([self.shared, self.pass0, self.pass1] + self.arriving)
+        self.wires.done(self.shared + [self.pass0, self.pass1] + self.arriving)
 
     def total(self, span):
         return (
@@ -755,9 +759,10 @@
 
         repeat(2, step)
 
+    rows_x = [PairGather(wires, spot, "x", second, own, s, n) for s, n in THREE]
     sums_y = [PairScatter(wires, spot, "y", part, got, passed, near, s, n) for s, n in THREE]
-    rows_x = [PairGather(wires, spot, "x", second, own, s, n) for s, n in THREE]
     repeat(2, lambda i: project_out(i, 1))
+    sums_y[0].share(1)
     for copy in kv_got:
         copy.wait_recv()
     cot_x[1].start()
@@ -768,7 +773,7 @@
     cot_x[1].rest()
     dn_line[0].forward()
     project_out(1 - c, 0)
-    sums_y[0].share()
+    sums_y[0].share(0)
     project_out(c, 0)
     for g in rows_y:
         g.close()
@@ -865,7 +870,7 @@
 
             @pl.when(k == 0)
             def _():
-                sums_x[i].shared.start()
+                sums_x[i].shared[0].start()
 
         repeat(2, step)
 
@@ -981,22 +986,20 @@
     grads_y[0].far()
     gather_back(2)
     grads_y[1].forward()
-    grad_down(0)
     grads_y[2].rest()
+    repeat(2, grad_down)
     grads_y[0].finish()
     mix_back(0)
     grads_y[1].near()
     grads_y[2].forward()
     gu_sum[0].second()
     gu_sum[1].first()
-    grad_down(1)
     grads_y[1].far()
+    repeat(4, down)
     grads_y[2].near()
-    repeat(2, down)
-    grads_y[2].far()
     grads_y[1].finish()
     mix_back(1)
-    repeat(2, lambda i: down(2 + i))
+    grads_y[2].far()
     tell(1, around(spot, "xy") + [spot.along("z", 1), spot.along("z", -1)])
     again = wires.move(normed_out, cots)
     gain_c[c, 1:2] = jnp.sum(total[...], axis=0, keepdims=True)
@@ -1040,8 +1043,8 @@
         for s, n in TWO
     ]
     sums_m[0].share()
+    repeat(2, lambda i: attend_back(i, 1))
     gu_sum[1].second()
-    repeat(2, lambda i: attend_back(i, 1))
     sums_m[0].first()
     sums_m[0].direct()
     sums_m[1].share()
@@ -1080,21 +1083,42 @@
         part[core, half * 2 : half * 2 + 2] = grad.reshape(2, OWN, D)
 
     sums_n = [PairScatter(wires, spot, "y", part, got, passed, near, s, n) for s, n in THREE]
-    gu_beside(1)
     repeat(4, lambda i: turn_back(i // 2, i % 2))
     repeat(2, lambda i: normed_back(i, 0))
+    for s in sums_n:
+        s.share(0)
+    gu_beside(1)
     for copy in far_got:
         copy.wait_recv()
     for core in (0, 1):
         grad_kv[core, 768:1024, :] += far_kv[core].astype(F32)
     repeat(4, lambda i: turn_back(i // 2, 2 + i % 2))
     normed_back(1 - c, 1)
-    share_all(sums_n)
+    for s in sums_n:
+        s.share(1)
     normed_back(c, 1)
     sums_n[0].first()
     sums_n[1].first()
     sums_n[2].first()
+    sums_m[0].through()
     dn_sum.second()
+
+    def out_rows_back(r, k):
+        unit = jnp.where(k < 128, k, k - 32)
+        real = (k < 96) | ((k >= 128) & (k < 224))
+        return real & (unit + ((unit * 5462) >> 16) * 4 == r)
+
+    grad_out = dot(mix[...].reshape(8 * OWN, 256), normed[...].reshape(8 * OWN, D), 0, 0)
+    grad_out = dot(picks(256, 256, out_rows_back), grad_out.astype(BF16), 1, 0)
+    wo[...] = grad_out.astype(BF16).reshape(4, 4, 16, D)
+    out_sum = LineScatter(
+        wires, spot, "z",
+        lambda pos, h: wo.at[pos, pl.ds(2 * h, 2)],
+        lambda h: ao.at[0, pl.ds(2 * h, 2)],
+        lambda h: ao.at[1, pl.ds(2 * h, 2)],
+        lambda side, h: ao.at[2 + side, pl.ds(2 * h, 2)],
+    )
+    out_sum.first(paced=True)
     again.wait()
 
     def grad_columns(i):
@@ -1117,24 +1141,9 @@
     gain_got = [wires.send(gain_c.at[c], gain_c.at[c], spot.sibling)]
     for s in sums_n:
         s.direct()
-    for s in sums_m:
-        s.through()
-
-    def out_rows_back(r, k):
-        unit = jnp.where(k < 128, k, k - 32)
-        real = (k < 96) | ((k >= 128) & (k < 224))
-        return real & (unit + ((unit * 5462) >> 16) * 4 == r)
-
-    grad_out = dot(mix[...].reshape(8 * OWN, 256), normed[...].reshape(8 * OWN, D), 0, 0)
-    grad_out = dot(picks(256, 256, out_rows_back), grad_out.astype(BF16), 1, 0)
-    wo[...] = grad_out.astype(BF16).reshape(4, 4, 16, D)
-    out_sum = LineScatter(
-        wires, spot, "z",
-        lambda pos, h: wo.at[pos, pl.ds(2 * h, 2)],
-        lambda h: ao.at[0, pl.ds(2 * h, 2)],
-        lambda h: ao.at[1, pl.ds(2 * h, 2)],
-        lambda side, h: ao.at[2 + side, pl.ds(2 * h, 2)],
-    )
+    sums_m[1].through()
+    out_sum.direct()
+    wires.done(left)
     hear(2, 4)
     att_sum = [
         LineScatter(
@@ -1152,11 +1161,8 @@
             lambda side, h: aq.at[2 + side, pl.ds(2 * h, 2), high],
         ),
     ]
-    for line in att_sum + [out_sum]:
+    for line in att_sum:
         line.first(paced=True)
-
-    for s in sums_n:
-        s.through()
 
     def add_gains(held, axis, into):
         for copy in gain_got:
@@ -1172,11 +1178,12 @@
         return [wires.send(into.at[me], into.at[me], spot.along(axis, by)) for by in (1, -1, 2)]
 
     gain_got = add_gains(gain_c, "x", gain_x)
-    for line in att_sum + [out_sum]:
+    for line in att_sum:
         line.direct()
-    wires.done(left)
-
-    for line in att_sum + [out_sum]:
+    out_sum.second()
+    for s in sums_n:
+        s.through()
+    for line in (att_sum[1], att_sum[0]):
         line.second()
     for copy in gu_got:
         copy.wait_recv()
@@ -1303,7 +1310,7 @@
 def layer_call(
     tokens, gain_attn, gain_mlp, cot, w_query, w_key, w_value, w_out, w_gate, w_up, w_down, marks
 ):
-    sends, receives = 120, 170
+    sends, receives = 110, 174
     shape = jax.ShapeDtypeStruct
     outs = (
         (shape((2, 4, OWN, D), BF16), ANY),

time: 171 us -> 166 us (0.971)
  Pallas kernels: 170 us -> 165 us
    pallas_call x1, Pallas kernels: 167 us -> 162 us  [layer_call(): pl.pallas_call(layer_kernel, out_shape=tuple((o[0] for o in outs)), in_sp...]
where the time goes in v4:
time: 166 us
  Pallas kernels  165 us (99%)
    pallas_call x1, Pallas kernels, layer_call(): pl.pallas_call(layer_kernel, out_shape=tuple((o[0] for o in outs)), in_sp...  162 us

profile of v4, /device:TPU:1, one launch (start us, length us, event | category | flops | bytes accessed | tf_op | source)
XLA Modules:
  0.0 165.8 jit_solution(1507304005666769925)
XLA Ops:
  0.6 162.1 %layer.1 = (bf16[2,4,192,1536]{3,2,1,0:T(8,128)(2,1)}, bf16[192,1536]{1,0:T(8,128)(2,1)}, bf16[192,1536]{1,0:T(8,128)(2,1)}, f32[2,1536]{1,0:T(2,128)}, bf16[96,...) custom-call(bf16[192,1536]{1,0:T(8,128)(2,1)} %tokens.1, ...), custom_call_target="tpu_custom_call" | custom-call | tf_op jit(solution)/shard_map/layer/pallas_call | solution.py:1371
  162.7 3.0 %finish.1 = (bf16[192,1536]{1,0:T(8,128)(2,1)}, bf16[192,1536]{1,0:T(8,128)(2,1)}, f32[12,128]{1,0:T(8,128)}, f32[12,128]{1,0:T(8,128)}, f32[96,192]{1,0:T(8,128...) custom-call(bf16[192,1536]{1,0:T(8,128)(2,1)} %get-tuple-element.30., ...), custom_call_target="tpu_custom_call" | custom-call | tf_op jit(solution)/shard_map/finish/pallas_call | solution.py:1400

commit v5 on v4

--- a/solution.py
+++ b/solution.py
@@ -437,6 +437,7 @@
 
 TWO = ((0, 96), (96, 96))
 THREE = ((0, 64), (64, 64), (128, 64))
+LOTS = ((0, 128), (128, 256))
 
 
 def dot(left, right, a, b):
@@ -683,6 +684,10 @@
         return wires.send(last, first, spot.along("x", 2))
 
     kv_got = [send_kv(c)]
+    for g in rows_y:
+        g.shared[3].wait_recv()
+    project(1 - c, turn(y, 2))
+    kv_got.append(send_kv(1 - c))
     dn_kept.wait()
     for copy in dn_side:
         copy.wait_recv()
@@ -691,10 +696,6 @@
         RingGather(wires, spot, "z", lambda pos, h: dn.at[pl.ds(2 * h, 2), pos, last_rows]),
     ]
     dn_line[1].begin()
-    for g in rows_y:
-        g.shared[3].wait_recv()
-    project(1 - c, turn(y, 2))
-    kv_got.append(send_kv(1 - c))
     normed_kept = wires.move(normed, normed_out)
     for piece in att_side + [out_side]:
         piece.close()
@@ -779,24 +780,22 @@
         g.close()
     normed_kept.wait()
     sums_y[0].first()
+    sums_y[0].left()
+    sums_y[0].direct()
     cot_x[1].forward()
     gu_line.rest()
+    sums_y[1].share()
+    sums_y[0].through()
     cot_x[0].far()
-    cot_x[0].finish()
-    sums_y[0].left()
-    sums_y[0].direct()
-    sums_y[1].share()
     cot_x[1].near()
-    sums_y[0].through()
+    sums_y[0].gone()
+    sums_y[1].first()
     gu_line.forward()
     cot_x[1].far()
-    sums_y[0].gone()
-    sums_y[1].first()
     sums_y[2].share()
     for line in dn_line:
         line.near()
         line.far()
-    cot_x[1].finish()
 
     def middle_rows(s):
         def use(span):
@@ -815,26 +814,25 @@
 
     gather_next(0)
     sums_y[1].direct()
-    back_hidden(0)
     sums_y[1].through()
     rows_x[0].rest()
-    grad_kv[...] = jnp.zeros_like(grad_kv)
-    wires.done(left)
+    cot_x[0].finish()
+    cot_x[1].finish()
+    back_hidden(0)
     rows_x[0].forward()
     sums_y[1].gone()
     sums_y[2].first()
+    grad_kv[...] = jnp.zeros_like(grad_kv)
+    wires.done(left)
     back_hidden(1)
     gather_next(1)
     sums_y[2].direct()
     rows_x[0].near()
-    back_hidden(2)
     sums_y[2].through()
     rows_x[1].rest()
+    back_hidden(2)
     rows_x[0].far()
     rows_x[1].forward()
-    gu_line.near()
-    gu_line.far()
-    rows_x[0].finish()
 
     def feed(core, i):
         start, part_size = THREE[i]
@@ -875,12 +873,16 @@
         repeat(2, step)
 
     gather_next(2)
+    gu_line.near()
+    gu_line.far()
+    rows_x[0].finish()
     early = wires.started()
     wires.again()
 
-    def grad_gate_up(i):
-        lanes = whole(i, 256)
-        rows = second[:, :, :, lanes].reshape(8 * OWN, 256)
+    def grad_gate_up(i, lot):
+        first, size = LOTS[lot]
+        lanes = pl.ds(pl.multiple_of(i * 384 + first, 128), size)
+        rows = second[:, :, :, lanes].reshape(8 * OWN, size)
         sent = work[:, :, :, 0:1024].reshape(8 * OWN, 1024)
         d_gu[lanes, :] = dot(rows, sent, 0, 0).astype(BF16)
 
@@ -954,22 +956,21 @@
     tell(0, [spot.along("z", 1), spot.along("z", -1)])
 
     grads_y[0].rest()
-    repeat(2, grad_gate_up)
-    grads_y[0].forward()
-    repeat(2, lambda i: grad_gate_up(2 + i))
-    sums_x[2].through()
-    gather_back(1)
-    grads_y[0].near()
-    repeat(2, lambda i: grad_gate_up(4 + i))
-    grads_y[1].rest()
+    repeat(4, lambda i: grad_gate_up(i, 0))
     hear(0, 2)
+    def lot_rows(base, lot, half=None):
+        first, size = LOTS[lot]
+        if half is None:
+            return pl.ds(pl.multiple_of(base + first, 64), size)
+        return pl.ds(pl.multiple_of(base + first + half * (size // 2), 64), size // 2)
+
     gu_sum = [
         LineScatter(
             wires, spot, "z",
-            lambda pos, h, lot=lot: d_gu.at[whole(pos * 4 + lot * 2 + h, 96)],
-            lambda h, lot=lot: gu.at[pl.ds(lot * 192 + h * 96, 96)],
-            lambda h, lot=lot: gu.at[pl.ds(384 + lot * 192 + h * 96, 96)],
-            lambda side, h, lot=lot: gu.at[pl.ds(768 + side * 384 + lot * 192 + h * 96, 96)],
+            lambda pos, h, lot=lot: d_gu.at[lot_rows(pos * 384, lot, h)],
+            lambda h, lot=lot: gu.at[lot_rows(0, lot, h)],
+            lambda h, lot=lot: gu.at[lot_rows(384, lot, h)],
+            lambda side, h, lot=lot: gu.at[lot_rows(768 + side * 384, lot, h)],
         )
         for lot in (0, 1)
     ]
@@ -978,11 +979,20 @@
     def gu_beside(lot):
         gu_sum[lot].finish()
         for by in (1, -1, 2):
-            part_of = d_gu.at[whole(z * 2 + lot, 192), whole(turn(y, by), 256)]
-            into = gu_in.at[y, pl.ds(lot * 192, 192)]
+            part_of = d_gu.at[lot_rows(z * 384, lot), whole(turn(y, by), 256)]
+            into = gu_in.at[y, pl.ds(*LOTS[lot])]
             gu_got.append(wires.send(part_of, into, spot.along("y", by)))
 
     gu_sum[0].first()
+    grads_y[0].forward()
+    sums_x[2].through()
+    repeat(2, lambda i: grad_gate_up(i, 1))
+    gather_back(1)
+    grads_y[0].near()
+    repeat(2, lambda i: grad_gate_up(2 + i, 1))
+    grads_y[1].rest()
+    gu_sum[0].second()
+    gu_sum[1].first()
     grads_y[0].far()
     gather_back(2)
     grads_y[1].forward()
@@ -992,13 +1002,13 @@
     mix_back(0)
     grads_y[1].near()
     grads_y[2].forward()
-    gu_sum[0].second()
-    gu_sum[1].first()
     grads_y[1].far()
     repeat(4, down)
+    gu_sum[1].second()
     grads_y[2].near()
     grads_y[1].finish()
     mix_back(1)
+    gu_beside(0)
     grads_y[2].far()
     tell(1, around(spot, "xy") + [spot.along("z", 1), spot.along("z", -1)])
     again = wires.move(normed_out, cots)
@@ -1034,7 +1044,6 @@
     for core in (0, 1):
         attend_back(core, 0)
         far_got.append(send_far(core))
-    gu_beside(0)
     hear(1, 7)
     sums_m = [
         PairScatter(
@@ -1044,7 +1053,6 @@
     ]
     sums_m[0].share()
     repeat(2, lambda i: attend_back(i, 1))
-    gu_sum[1].second()
     sums_m[0].first()
     sums_m[0].direct()
     sums_m[1].share()
@@ -1083,11 +1091,11 @@
         part[core, half * 2 : half * 2 + 2] = grad.reshape(2, OWN, D)
 
     sums_n = [PairScatter(wires, spot, "y", part, got, passed, near, s, n) for s, n in THREE]
+    gu_beside(1)
     repeat(4, lambda i: turn_back(i // 2, i % 2))
     repeat(2, lambda i: normed_back(i, 0))
     for s in sums_n:
         s.share(0)
-    gu_beside(1)
     for copy in far_got:
         copy.wait_recv()
     for core in (0, 1):

time: 166 us -> 164 us (0.988)
  Pallas kernels: 165 us -> 163 us
    pallas_call x1, Pallas kernels: 162 us -> 160 us  [layer_call(): pl.pallas_call(layer_kernel, out_shape=tuple((o[0] for o in outs)), in_sp...]
where the time goes in v5:
time: 164 us
  Pallas kernels  163 us (99%)
    pallas_call x1, Pallas kernels, layer_call(): pl.pallas_call(layer_kernel, out_shape=tuple((o[0] for o in outs)), in_sp...  160 us

profile of v5, /device:TPU:1, one launch (start us, length us, event | category | flops | bytes accessed | tf_op | source)
XLA Modules:
  0.0 164.0 jit_solution(12552018296975805476)
XLA Ops:
  0.6 160.3 %layer.1 = (bf16[2,4,192,1536]{3,2,1,0:T(8,128)(2,1)}, bf16[192,1536]{1,0:T(8,128)(2,1)}, bf16[192,1536]{1,0:T(8,128)(2,1)}, f32[2,1536]{1,0:T(2,128)}, bf16[96,...) custom-call(bf16[192,1536]{1,0:T(8,128)(2,1)} %tokens.1, ...), custom_call_target="tpu_custom_call" | custom-call | tf_op jit(solution)/shard_map/layer/pallas_call | solution.py:1379
  161.0 3.0 %finish.1 = (bf16[192,1536]{1,0:T(8,128)(2,1)}, bf16[192,1536]{1,0:T(8,128)(2,1)}, f32[12,128]{1,0:T(8,128)}, f32[12,128]{1,0:T(8,128)}, f32[96,192]{1,0:T(8,128...) custom-call(bf16[192,1536]{1,0:T(8,128)(2,1)} %get-tuple-element.30., ...), custom_call_target="tpu_custom_call" | custom-call | tf_op jit(solution)/shard_map/finish/pallas_call | solution.py:1408

commit v6 on v5

--- a/solution.py
+++ b/solution.py
@@ -1191,6 +1191,10 @@
     out_sum.second()
     for s in sums_n:
         s.through()
+    dn_sum.finish()
+    dn_got = [
+        wires.send(d_dn.at[turn(y, by), z], dn_in.at[y], spot.along("y", by)) for by in (1, -1, 2)
+    ]
     for line in (att_sum[1], att_sum[0]):
         line.second()
     for copy in gu_got:
@@ -1232,10 +1236,6 @@
         s.arrive()
         over_rows(s.start_row, s.size, result_rows(s))
 
-    dn_sum.finish()
-    dn_got = [
-        wires.send(d_dn.at[turn(y, by), z], dn_in.at[y], spot.along("y", by)) for by in (1, -1, 2)
-    ]
     for s in sums_m:
         result_part(s)
     result_kept = wires.move(second.at[c, x], result_out)

time: 164 us -> 164 us (level)
  no operation moved by 1% of the time
where the time goes in v6:
time: 164 us
  Pallas kernels  163 us (99%)
    pallas_call x1, Pallas kernels, layer_call(): pl.pallas_call(layer_kernel, out_shape=tuple((o[0] for o in outs)), in_sp...  160 us

profile of v6, /device:TPU:1, one launch (start us, length us, event | category | flops | bytes accessed | tf_op | source)
XLA Modules:
  0.0 164.0 jit_solution(8477222110515905909)
XLA Ops:
  0.6 160.3 %layer.1 = (bf16[2,4,192,1536]{3,2,1,0:T(8,128)(2,1)}, bf16[192,1536]{1,0:T(8,128)(2,1)}, bf16[192,1536]{1,0:T(8,128)(2,1)}, f32[2,1536]{1,0:T(2,128)}, bf16[96,...) custom-call(bf16[192,1536]{1,0:T(8,128)(2,1)} %tokens.1, ...), custom_call_target="tpu_custom_call" | custom-call | tf_op jit(solution)/shard_map/layer/pallas_call | solution.py:1379
  161.0 3.0 %finish.1 = (bf16[192,1536]{1,0:T(8,128)(2,1)}, bf16[192,1536]{1,0:T(8,128)(2,1)}, f32[12,128]{1,0:T(8,128)}, f32[12,128]{1,0:T(8,128)}, f32[96,192]{1,0:T(8,128...) custom-call(bf16[192,1536]{1,0:T(8,128)(2,1)} %get-tuple-element.30., ...), custom_call_target="tpu_custom_call" | custom-call | tf_op jit(solution)/shard_map/finish/pallas_call | solution.py:1408
